TPU v7x, 32 devices: a whole 2x2x4 slice. The times are simulated.
32 devices in a mesh: dp: 16 (over z, y, x), mp: 2 (over core).
Axes of the slice: x: 2, y: 2, z: 4, core: 2. Of those that a mesh axis runs over, the one named last changes fastest.
Arguments:
- series: bfloat16 [896, 32, 336], P('mp', 'dp'), may hold values from -6 to 6
- groups: int32 [32], P('dp'), may hold values from 0 to 2
- counts: int32 [32], P('dp'), may hold values from 574 to 862, as said below
- cotangent: bfloat16 [896, 32, 512], P('mp', 'dp'), may hold values from -18 to 18
- embed_weight: float32 [3, 336, 512], replicated, may hold values from -0.3125 to 0.3125
- embed_moment: float32 [3, 336, 512], replicated, may hold values from -6 to 6
- embed_error: float32 [16, 3, 336, 512], P('dp'), may hold values from -80 to 80
- embed_start: float32 [512, 8], replicated, may hold values from -6 to 6
- attend_weight: float32 [512, 3, 512], P(None, None, 'mp'), may hold values from -0.25 to 0.25
- attend_moment: float32 [512, 3, 512], P(None, None, 'mp'), may hold values from -6 to 6
- attend_error: float32 [16, 512, 3, 512], P('dp', None, None, 'mp'), may hold values from -80 to 80
- attend_start: float32 [3, 512, 8], P(None, 'mp'), may hold values from -6 to 6
- mixer_weight: float32 [512, 512], P('mp'), may hold values from -2 to 2
- mixer_moment: float32 [512, 512], P('mp'), may hold values from -6 to 6
- mixer_error: float32 [16, 512, 512], P('dp', 'mp'), may hold values from -80 to 80
- mixer_start: float32 [2, 512, 8], P('mp'), may hold values from -6 to 6
- inner_weight: float32 [512, 2048], P(None, 'mp'), may hold values from -0.25 to 0.25
- inner_moment: float32 [512, 2048], P(None, 'mp'), may hold values from -6 to 6
- inner_error: float32 [16, 512, 2048], P('dp', None, 'mp'), may hold values from -80 to 80
- inner_start: float32 [2048, 8], P('mp'), may hold values from -6 to 6
- outer_weight: float32 [2048, 512], P('mp'), may hold values from -0.125 to 0.125
- outer_moment: float32 [2048, 512], P('mp'), may hold values from -6 to 6
- outer_error: float32 [16, 2048, 512], P('dp', 'mp'), may hold values from -80 to 80
- outer_start: float32 [2, 512, 8], P('mp'), may hold values from -6 to 6
- embed_bias: float32 [3, 512], replicated, may hold values from -1.75 to 1.75
- embed_bias_moment: float32 [3, 512], replicated, may hold values from -6 to 6
- query_bias: float32 [2, 512], P(None, 'mp'), may hold values from -1.75 to 1.75
- query_bias_moment: float32 [2, 512], P(None, 'mp'), may hold values from -6 to 6
- inner_bias: float32 [2048], P('mp'), may hold values from -1.75 to 1.75
- inner_bias_moment: float32 [2048], P('mp'), may hold values from -6 to 6
- norm_gains: float32 [2, 512], replicated, may hold values from 0.5 to 1.5
- gains_moment: float32 [2, 512], replicated, may hold values from -6 to 6
- shared_biases: float32 [4, 512], replicated, may hold values from -1.75 to 1.75
- biases_moment: float32 [4, 512], replicated, may hold values from -6 to 6
Outputs:
- output: float32 [896, 32, 512], P('mp', 'dp')
- series_grad: float32 [896, 32, 336], P('mp', 'dp')
- embed_weight_new: float32 [3, 336, 512], replicated
- embed_moment_new: float32 [3, 336, 512], replicated
- embed_error_new: float32 [16, 3, 336, 512], P('dp')
- embed_left: float32 [3, 336, 8], replicated
- embed_right: float32 [512, 8], replicated
- attend_weight_new: float32 [512, 3, 512], P(None, None, 'mp')
- attend_moment_new: float32 [512, 3, 512], P(None, None, 'mp')
- attend_error_new: float32 [16, 512, 3, 512], P('dp', None, None, 'mp')
- attend_left: float32 [2, 512, 8], P('mp')
- attend_right: float32 [3, 512, 8], P(None, 'mp')
- mixer_weight_new: float32 [512, 512], P('mp')
- mixer_moment_new: float32 [512, 512], P('mp')
- mixer_error_new: float32 [16, 512, 512], P('dp', 'mp')
- mixer_left: float32 [512, 8], P('mp')
- mixer_right: float32 [2, 512, 8], P('mp')
- inner_weight_new: float32 [512, 2048], P(None, 'mp')
- inner_moment_new: float32 [512, 2048], P(None, 'mp')
- inner_error_new: float32 [16, 512, 2048], P('dp', None, 'mp')
- inner_left: float32 [2, 512, 8], P('mp')
- inner_right: float32 [2048, 8], P('mp')
- outer_weight_new: float32 [2048, 512], P('mp')
- outer_moment_new: float32 [2048, 512], P('mp')
- outer_error_new: float32 [16, 2048, 512], P('dp', 'mp')
- outer_left: float32 [2048, 8], P('mp')
- outer_right: float32 [2, 512, 8], P('mp')
- embed_bias_moment_new: float32 [3, 512], replicated
- embed_bias_new: float32 [3, 512], replicated
- query_bias_moment_new: float32 [2, 512], P(None, 'mp')
- query_bias_new: float32 [2, 512], P(None, 'mp')
- inner_bias_moment_new: float32 [2048], P('mp')
- inner_bias_new: float32 [2048], P('mp')
- gains_moment_new: float32 [2, 512], replicated
- norm_gains_new: float32 [2, 512], replicated
- biases_moment_new: float32 [4, 512], replicated
- shared_biases_new: float32 [4, 512], replicated
Inputs may be any that keep to these rules, and one draw needn't show every extreme that they name: `counts`: some window has exactly 862 live variates.
All inputs are finite; a program needn't handle non-finite values.
Results may differ from a plain program's by a relative error of at most 0.02.
Values may be sent and summed in bfloat16 or wider, within the bound.
A program may use at most 256 MiB of HBM per device.

v0:
```python
import functools
import math

import jax
import jax.numpy as jnp
from jax import lax
from jax.experimental import pallas as pl
from jax.experimental.pallas import tpu as pltpu
from jax.sharding import PartitionSpec as P

HEADS = 8
momentum_decay = 0.9
norm_epsilon = 1e-05
base_rate = 0.03
inverse_root_two = 0.7071067811865476
inverse_root_tau = 0.3989422804014327
log2_e = 1.4426950408889634
ln_two = 0.6931471805599453
f32 = jnp.float32
bf16 = jnp.bfloat16
VMEM = pltpu.VMEM
VM = pl.BlockSpec(memory_space=pltpu.VMEM)
SM = pl.BlockSpec(memory_space=pltpu.SMEM)
MIB = 1024 * 1024


def dot_nn(a, b):
    return lax.dot_general(a, b, (((1,), (0,)), ((), ())), preferred_element_type=f32)


def dot_nt(a, b):
    return lax.dot_general(a, b, (((1,), (1,)), ((), ())), preferred_element_type=f32)


def dot_tn(a, b):
    return lax.dot_general(a, b, (((0,), (0,)), ((), ())), preferred_element_type=f32)


def split_two(x):
    high = x.astype(bf16)
    return high, (x - high.astype(f32)).astype(bf16)


def three_way(x, lane):
    high = x.astype(bf16).astype(f32)
    rest = x - high
    middle = rest.astype(bf16).astype(f32)
    last = rest - middle
    place = lax.rem(lane, 3)
    return jnp.where(place == 0, high, jnp.where(place == 1, middle, last)).astype(bf16)


LIMITS = (20, 24, 32, 48, 40, 40, 24, 20, 56)
TILES = 4


def place_and_count(counts):
    position = lax.axis_index("mp")
    return position, counts[position]


def row_number(rows, position):
    half = rows // 2
    index = lax.broadcasted_iota(jnp.int32, (rows, 128), 0)
    return jnp.where(index < half, index + position * half, index - half + (1 - position) * half)


def lookback_of(group, history):
    return jnp.where(
        group == 0, history * 2 // 7, jnp.where(group == 1, history * 4 // 7, history)
    ).astype(jnp.int32)


def split_pair(pair_ref, mine, theirs, columns):
    position = lax.axis_index("mp")

    @pl.when(position == 0)
    def _():
        mine[:, columns] = pair_ref[:, 0, :]
        theirs[:, columns] = pair_ref[:, 1, :]

    @pl.when(position != 0)
    def _():
        mine[:, columns] = pair_ref[:, 1, :]
        theirs[:, columns] = pair_ref[:, 0, :]


def join_pair(mine, theirs, pair_ref):
    position = lax.axis_index("mp")

    @pl.when(position == 0)
    def _():
        pair_ref[:, 0, :] = mine[...]
        pair_ref[:, 1, :] = theirs[...]

    @pl.when(position != 0)
    def _():
        pair_ref[:, 1, :] = mine[...]
        pair_ref[:, 0, :] = theirs[...]


def prepare_attention(
    groups, series, attend, embed, embed_bias, query_bias, inner_bias,
    send, series_own, table, bias_row, small,
):
    half, _, history = series.shape
    depth = attend.shape[1] // 2
    send[:half, 256:] = jnp.zeros((half, send.shape[1] - 256), bf16)
    split_pair(series, series_own, send.at[:half], slice(0, history))
    for kind in range(3):
        rows = slice(half + kind * depth, half + (kind + 1) * depth)
        send[rows, :256] = attend[kind, :depth, :].astype(bf16)
        send[rows, 256:] = attend[kind, depth:, :].astype(bf16)
    group = groups[lax.axis_index("mp")]
    chosen = embed[group]
    row = lax.broadcasted_iota(jnp.int32, chosen.shape, 0)
    table[...] = jnp.where(row >= history - lookback_of(group, history), chosen, 0.0).astype(bf16)
    row = lax.broadcasted_iota(jnp.int32, embed_bias.shape, 0)
    bias_row[...] = jnp.sum(jnp.where(row == group, embed_bias[...], 0.0), axis=0, keepdims=True)
    small[...] = jnp.zeros_like(small)
    small[0:2, : query_bias.shape[1]] = query_bias[...]
    small[2:3, :] = inner_bias[...]


def prepare_feed(cotangent, mixer, inner, outer, send, cot_own):
    half = cotangent.shape[0]
    m, d = mixer.shape[0], inner.shape[0]
    o = outer.shape[0]
    send[:m] = mixer[...].astype(bf16)
    send[m : m + d] = inner[:, :512].astype(bf16)
    send[m + d : m + 2 * d] = inner[:, 512:].astype(bf16)
    send[m + 2 * d : m + 2 * d + o] = outer[...].astype(bf16)
    split_pair(cotangent, cot_own, send.at[m + 2 * d + o :], slice(None))


def attend_block(pack, half, kind):
    start = half + kind * 256
    return jnp.concatenate([pack[start : start + 256, :256], pack[start : start + 256, 256:]], axis=0)


def attend_forward(
    counts, series_own, table, embed_bias, own, other, small, small_other,
    hidden_ref, token_ref, query_ref, key_ref, value_ref, context_ref, lse_ref,
):
    rows, width = hidden_ref.shape
    half, history = series_own.shape
    part = width // 2
    head_dim = width // HEADS
    position, count = place_and_count(counts)
    for index, block in enumerate((series_own[...], other[:half, :history])):
        values = dot_nn(block, table[...]) + embed_bias[...]
        hidden_ref[pl.ds(index * half, half), :] = values
        token_ref[pl.ds(index * half, half), :] = values.astype(bf16)
    scale = head_dim**-0.5 * log2_e
    tokens = token_ref[...]
    for index, (pack, bias) in enumerate(((own, small), (other, small_other))):
        columns = pl.ds(index * part, part)
        query_ref[:, columns] = (
            (dot_nn(tokens, attend_block(pack, half, 0)) + bias[0:1, :part]) * scale
        ).astype(bf16)
        key_ref[:, columns] = dot_nn(tokens, attend_block(pack, half, 1)).astype(bf16)
        value_ref[:, columns] = (
            dot_nn(tokens, attend_block(pack, half, 2)) + bias[1:2, :part]
        ).astype(bf16)
    lane = lax.broadcasted_iota(jnp.int32, (rows, 128), 1)
    dead = row_number(rows, position) >= count
    extra_query = jnp.where(lane == 0, 1.0, 0.0).astype(bf16)
    extra_key = jnp.where((lane == 0) & dead, -1e30, 0.0).astype(bf16)
    ones = jnp.ones((rows, 128), bf16)
    lse_ref[...] = jnp.zeros_like(lse_ref)

    def pair(index, carry):
        columns = pl.ds(pl.multiple_of(index * 128, 128), 128)
        queries = query_ref[:, columns]
        keys = jnp.concatenate([key_ref[:, columns], extra_key], axis=1)
        values = jnp.concatenate([value_ref[:, columns], ones], axis=1)
        found = []
        for side in range(2):
            mine = (lane >= head_dim) if side else (lane < head_dim)
            query = jnp.concatenate(
                [jnp.where(mine, queries, jnp.zeros_like(queries)), extra_query], axis=1
            )
            scores = dot_nt(query, keys)
            peak = jnp.max(scores, axis=1, keepdims=True)
            soft = jnp.exp2(scores - peak).astype(bf16)
            mixed = dot_nn(soft, values)
            total = mixed[:, 128:]
            found.append(mixed[:, :128] / total)
            log_total = jnp.broadcast_to(peak, (rows, 128)) + jnp.log2(total)
            lse_ref[...] = jnp.where(lane // 3 == index * 2 + side, log_total, lse_ref[...])
        context_ref[:, columns] = jnp.where(lane < head_dim, found[0], found[1]).astype(bf16)
        return carry

    lax.fori_loop(0, width // 128, pair, 0)


def norm_rows(values, gain, shift):
    centered = values - jnp.mean(values, axis=-1, keepdims=True)
    inverse = lax.rsqrt(jnp.mean(centered * centered, axis=-1, keepdims=True) + norm_epsilon)
    unit = centered * inverse
    return unit * gain + shift, unit, inverse


def norm_rows_back(upstream, unit, inverse, gain):
    scaled = upstream * gain
    return inverse * (
        scaled
        - jnp.mean(scaled, axis=-1, keepdims=True)
        - unit * jnp.mean(scaled * unit, axis=-1, keepdims=True)
    )


def feed_forward(
    tiles, counts, context_ref, hidden_ref, own, other, small, small_other, gains, biases, cot_own,
    output_ref, output_send, active_ref, preact_ref, normed_ref, feed_ref, attend_ref, resid_ref,
    context_grad_ref, delta_ref, sums_ref, inner_sum_ref, grads_send, slope_ref,
):
    rows, width = hidden_ref.shape
    tile = rows // tiles
    half = rows // 2
    part = width // 2
    units = active_ref.shape[1]
    inner_part = units // 2
    chunk = 512
    position, count = place_and_count(counts)
    sums_ref[...] = jnp.zeros_like(sums_ref)
    inner_sum_ref[...] = jnp.zeros_like(inner_sum_ref)
    at_inner = part
    at_outer = part + inner_part
    at_cot = at_outer + inner_part

    def inner_chunk(index):
        pack = (own, other)[index * chunk // inner_part]
        start = at_inner + (index * chunk % inner_part) // chunk * width
        return pack[start : start + width, :]

    def outer_chunk(index):
        pack = (own, other)[index * chunk // inner_part]
        start = at_outer + index * chunk % inner_part
        return pack[start : start + chunk, :]

    head_dim = width // HEADS
    head = lax.broadcasted_iota(jnp.int32, (width, 128), 0) // head_dim
    lane = lax.broadcasted_iota(jnp.int32, (width, 128), 1)
    chooser = jnp.where(lane // 3 == head, -1.0, 0.0).astype(bf16)

    def add(row, values):
        sums_ref[row : row + 1, :] += jnp.sum(values, axis=0, keepdims=True)

    def one_tile(step, carry):
        place = pl.ds(pl.multiple_of(step * tile, tile), tile)
        context = context_ref[place, :]
        attended = dot_nn(context[:, :part], own[:part, :]) + dot_nn(
            context[:, part:], other[:part, :]
        )
        normed, unit_one, inverse_one = norm_rows(
            hidden_ref[place, :] + attended + biases[2:3, :], gains[0:1, :], biases[0:1, :]
        )
        normed_low = normed.astype(bf16)
        normed_ref[place, :] = normed_low
        for index in range(units // chunk):
            columns = slice(index * chunk, (index + 1) * chunk)
            bias = (small, small_other)[index * chunk // inner_part]
            start = index * chunk % inner_part
            preact = dot_nn(normed_low, inner_chunk(index)) + bias[2:3, start : start + chunk]
            phi = 0.5 + 0.5 * lax.erf(preact * inverse_root_two)
            active_ref[place, columns] = (preact * phi).astype(bf16)
            slope_ref[:, columns] = (
                phi + preact * jnp.exp2(preact * preact * (-0.5 * log2_e)) * inverse_root_tau
            ).astype(bf16)
        feed_out = dot_nn(active_ref[place, :inner_part], own[at_outer:at_cot, :]) + dot_nn(
            active_ref[place, inner_part:], other[at_outer:at_cot, :]
        )
        output, unit_two, inverse_two = norm_rows(
            normed + feed_out + biases[3:4, :], gains[1:2, :], biases[1:2, :]
        )
        index = lax.broadcasted_iota(jnp.int32, (tile, width), 0)

        @pl.when(step < tiles // 2)
        def _():
            output_ref[place, :] = output
        far = step - tiles // 2
        far_place = pl.ds(pl.multiple_of(jnp.maximum(far, 0) * tile, tile), tile)
        near_place = pl.ds(pl.multiple_of(jnp.minimum(step, tiles // 2 - 1) * tile, tile), tile)

        @pl.when(step >= tiles // 2)
        def _():
            output_send[far_place, :] = output
        cot = jnp.where(
            step < tiles // 2,
            cot_own[near_place, :],
            other[pl.ds(pl.multiple_of(at_cot + jnp.maximum(far, 0) * tile, 32), tile), :],
        ).astype(f32)
        first = jnp.where(
            step < tiles // 2,
            position * half + step * tile,
            (1 - position) * half + far * tile,
        )
        upstream = jnp.where(index + first < count, cot, 0.0)
        resid_two = norm_rows_back(upstream, unit_two, inverse_two, gains[1:2, :])
        feed_grad = resid_two.astype(bf16)
        feed_ref[place, :] = feed_grad
        for index in range(units // chunk):
            columns = slice(index * chunk, (index + 1) * chunk)
            grad = dot_nt(feed_grad, outer_chunk(index))
            preact_ref[place, columns] = (grad * slope_ref[:, columns].astype(f32)).astype(bf16)
        normed_grad = resid_two
        for index in range(units // chunk):
            columns = slice(index * chunk, (index + 1) * chunk)
            normed_grad = normed_grad + dot_nt(preact_ref[place, columns], inner_chunk(index))
        resid_one = norm_rows_back(normed_grad, unit_one, inverse_one, gains[0:1, :])
        resid_ref[place, :] = resid_one
        attend_grad = resid_one.astype(bf16)
        attend_ref[place, :] = attend_grad
        context_grad = jnp.concatenate(
            [dot_nt(attend_grad, own[:part, :]), dot_nt(attend_grad, other[:part, :])], axis=1
        ).astype(bf16)
        context_grad_ref[place, :] = context_grad
        high, low = split_two(context_grad.astype(f32) * context.astype(f32))
        delta = dot_nn(high, chooser) + dot_nn(low, chooser)
        delta_ref[place, :] = three_way(delta, lax.broadcasted_iota(jnp.int32, (tile, 128), 1))
        add(1, normed_grad * unit_one)
        add(2, upstream * unit_two)
        add(3, normed_grad)
        add(4, upstream)
        add(5, resid_one)
        add(6, resid_two)
        inner_sum_ref[0:1, :] += jnp.sum(preact_ref[place, :].astype(f32), axis=0, keepdims=True)
        return carry

    lax.fori_loop(0, tiles, one_tile, 0)
    grads_send[:inner_part, :] = dot_tn(active_ref[:, inner_part:], feed_ref[...]).astype(bf16)
    for index in range(inner_part // chunk):
        start = inner_part + index * chunk
        grads_send[inner_part + index * width : inner_part + (index + 1) * width, :] = dot_tn(
            normed_ref[...], preact_ref[:, start : start + chunk]
        ).astype(bf16)
    grads_send[2 * inner_part :, :] = dot_tn(context_ref[:, part:], attend_ref[...]).astype(bf16)


def attend_backward(
    groups, counts, query_ref, key_ref, value_ref, lse_ref, context_grad_ref, delta_ref,
    token_ref, resid_ref, own, other, table, series_own, sums_ref, inner_sum_ref,
    attend_own, send, series_near, series_far, near_out, far_out,
    dquery_ref, dkey_ref, dvalue_ref,
):
    rows, width = query_ref.shape
    head_dim = width // HEADS
    half, history = series_own.shape
    part = width // 2
    position, count = place_and_count(counts)
    lane = lax.broadcasted_iota(jnp.int32, (rows, 128), 1)
    dead = row_number(rows, position) >= count
    extra_query = jnp.where(lane == 127, jnp.ones((rows, 128), bf16), three_way(-lse_ref[...], lane))
    extra_key = jnp.where((lane == 127) & dead, -1e30, 0.0)
    extra_grad = delta_ref[...]

    def pair(index, carry):
        columns = pl.ds(pl.multiple_of(index * 128, 128), 128)
        queries = query_ref[:, columns]
        keys = key_ref[:, columns]
        values = value_ref[:, columns]
        grads = context_grad_ref[:, columns]
        dquery = dkey = dvalue = None
        for side in range(2):
            mine = (lane >= head_dim) if side else (lane < head_dim)
            hot = lane // 3 == index * 2 + side
            nothing = jnp.zeros_like(queries)
            query = jnp.where(mine, queries, nothing)
            grad = jnp.where(mine, grads, nothing)
            key = jnp.where(mine, keys, nothing)
            soft = jnp.exp2(
                dot_nt(
                    jnp.concatenate([keys, jnp.where(hot, 1.0, extra_key).astype(bf16)], axis=1),
                    jnp.concatenate([query, extra_query], axis=1),
                )
            )
            centered = dot_nt(
                jnp.concatenate([values, jnp.where(hot, 1.0, 0.0).astype(bf16)], axis=1),
                jnp.concatenate([grad, extra_grad], axis=1),
            )
            score_grad = (soft * centered).astype(bf16)
            one = dot_nn(soft.astype(bf16), grad)
            two = dot_nn(score_grad, query)
            three = dot_tn(key, score_grad)
            dvalue = one if dvalue is None else dvalue + one
            dkey = two if dkey is None else dkey + two
            dquery = three if dquery is None else dquery + three
        dvalue_ref[:, columns] = dvalue.astype(bf16)
        dkey_ref[:, columns] = (dkey * ln_two).astype(bf16)
        dquery_ref[:, columns] = (dquery.T * head_dim**-0.5).astype(bf16)
        return carry

    lax.fori_loop(0, width // 128, pair, 0)

    tokens = token_ref[...]
    total = resid_ref[...]
    near_out[...] = jnp.zeros_like(near_out)
    far_out[...] = jnp.zeros_like(far_out)
    for kind, grad_ref in enumerate((dquery_ref, dkey_ref, dvalue_ref)):
        low = grad_ref[...]
        attend_own[kind] = dot_tn(tokens, low[:, :part])
        far = dot_tn(tokens, low[:, part:]).astype(bf16)
        send[kind * part : (kind + 1) * part, :part] = far[:part]
        send[kind * part : (kind + 1) * part, part:] = far[part:]
        total = (
            total
            + dot_nt(low[:, :part], attend_block(own, half, kind))
            + dot_nt(low[:, part:], attend_block(other, half, kind))
        )
        if kind != 1:
            column = jnp.sum(low.astype(f32), axis=0, keepdims=True)
            start = kind // 2 * part
            near_out[7:8, start : start + part] = column[:, :part]
            far_out[7:8, start : start + part] = column[:, part:]
    low = total.astype(bf16)
    series_near[...] = dot_nt(low[:half], table[...])
    series_far[...] = dot_nt(low[half:], table[...])
    table_grad = dot_tn(series_own[...], low[:half]) + dot_tn(other[:half, :history], low[half:])
    row = lax.broadcasted_iota(jnp.int32, table_grad.shape, 0)
    seen = row >= history - lookback_of(groups[position], history)
    send[3 * part :, :] = jnp.where(seen, table_grad, 0.0).astype(bf16)
    shared = sums_ref[0:7, :]
    bias_grad = jnp.sum(low.astype(f32), axis=0, keepdims=True)
    near_out[0:7, :] = shared
    far_out[0:7, :] = shared
    near_out[0:1, :] = bias_grad
    far_out[0:1, :] = bias_grad
    count_near = inner_sum_ref.shape[1] // 2 // width
    for index in range(count_near):
        near_out[8 + index : 9 + index, :] = inner_sum_ref[0:1, index * width : (index + 1) * width]
        far_out[8 + index : 9 + index, :] = inner_sum_ref[
            0:1, (count_near + index) * width : (count_near + index + 1) * width
        ]


def left_product(start, matrix):
    start_high, start_low = split_two(start)
    high, low = split_two(matrix)
    both = dot_nt(jnp.concatenate([start_high, start_low], axis=0), high)
    return both[:8] + both[8:] + dot_nt(start_high, low)


def right_product(basis, matrix):
    basis_high, basis_low = split_two(basis)
    high, low = split_two(matrix)
    both = dot_nn(jnp.concatenate([basis_high, basis_low], axis=0), high)
    return both[:8] + both[8:] + dot_nn(basis_high, low)


def feed_matrices(
    active_ref, preact_ref, normed_ref, feed_ref, context_ref, attend_ref, received,
    e_outer, e_inner, e_mixer, s_outer, s_inner, s_mixer, output_near, output_far,
    outer, inner, mixer, left, output,
):
    width = feed_ref.shape[1]
    inner_part = outer.shape[0]
    part = mixer.shape[0]
    chunk = 512
    join_pair(output_near, output_far, output)
    outer[...] = (
        dot_tn(active_ref[:, :inner_part], feed_ref[...])
        + received[:inner_part, :].astype(f32)
        + e_outer[...]
    )
    for index in range(inner_part // chunk):
        columns = slice(index * chunk, (index + 1) * chunk)
        start = inner_part + index * width
        inner[:, columns] = (
            dot_tn(normed_ref[...], preact_ref[:, columns])
            + received[start : start + width, :].astype(f32)
            + e_inner[:, columns]
        )
    mixer[...] = (
        dot_tn(context_ref[:, :part], attend_ref[...])
        + received[2 * inner_part :, :].astype(f32)
        + e_mixer[...]
    )
    left[:, 0:1024] = left_product(s_outer[...], outer[...])
    left[:, 1024:1536] = left_product(s_inner[...], inner[...])
    left[:, 1536:1792] = left_product(s_mixer[...], mixer[...])


def other_matrices(
    groups, near_attend, own, received, e_attend, e_embed, s_attend, s_embed, left_part, near, far,
    series_near, series_far,
    attend, embed, left, series_grad,
):
    part = near_attend.shape[2]
    position = lax.axis_index("mp")
    join_pair(series_near, series_far, series_grad)
    total = None
    for kind in range(3):
        rows = slice(kind * part, (kind + 1) * part)
        block = jnp.concatenate([received[rows, :part], received[rows, part:]], axis=0)
        attend[kind] = near_attend[kind] + block.astype(f32) + e_attend[kind]
        term = left_product(s_attend[kind], attend[kind])
        total = term if total is None else total + term
    mine, theirs = groups[position], groups[1 - position]
    table_near = own[3 * part :, :].astype(f32)
    table_far = received[3 * part :, :].astype(f32)
    pieces = []
    for group in range(embed.shape[0]):
        grad = jnp.where(mine == group, table_near, 0.0) + jnp.where(theirs == group, table_far, 0.0)
        embed[group] = grad + e_embed[group]
        pieces.append(left_product(s_embed[...], embed[group]))
    used = embed.shape[0] * embed.shape[1]
    left[:, 0:1024] = jnp.concatenate(pieces + [jnp.zeros((8, 1024 - used), f32)], axis=1)
    left[:, 1024:2048] = left_part[:, 0:1024]
    left[:, 2048:2560] = total
    left[:, 2560:3328] = left_part[:, 1024:1792]
    common = near[1:7, :] + far[1:7, :]
    row = lax.broadcasted_iota(jnp.int32, (3, near.shape[1]), 0)
    bias = jnp.where(row == mine, near[0:1, :], 0.0) + jnp.where(row == theirs, far[0:1, :], 0.0)
    left[:, 3328:3840] = jnp.concatenate([bias, common[:5]], axis=0)
    rest = jnp.concatenate([common[5:6], near[7:10, :] + far[7:10, :]], axis=0)
    for row in range(4):
        left[2 * row : 2 * row + 1, 3840:4096] = rest[row : row + 1, :256]
        left[2 * row + 1 : 2 * row + 2, 3840:4096] = rest[row : row + 1, 256:]


def orthonormal_rows(vectors):
    rank = vectors.shape[0]
    row = lax.broadcasted_iota(jnp.int32, vectors.shape, 0)
    for index in range(rank):
        pivot = vectors[index : index + 1, :]
        inner = jnp.sum(vectors * pivot, axis=1, keepdims=True)
        size = inner[index : index + 1, :] + 1e-12
        reduced = vectors - pivot * (inner / size)
        vectors = jnp.where(
            row > index, reduced, jnp.where(row == index, vectors * lax.rsqrt(size), vectors)
        )
    return vectors


def reduce_factors(
    replicas, start_ref, embed, outer, attend, inner, mixer,
    left_ref, right_ref, mean_ref,
    summed, partial, gathered, parts_one, parts_two, send_sems, recv_sems,
):
    me = lax.axis_index("dp")
    barrier = pltpu.get_barrier_semaphore()
    chunk = start_ref.shape[1] // replicas
    share = 1.0 / replicas

    def peer(offset):
        return lax.rem(me + offset, replicas)

    def columns(index):
        return pl.ds(pl.multiple_of(index * chunk, 128), chunk)

    def each(what):
        def body(offset, carry):
            what(offset)
            return carry

        lax.fori_loop(1, replicas, body, 0)

    each(
        lambda offset: pl.semaphore_signal(
            barrier, inc=1, device_id={"dp": peer(offset)}, device_id_type=pl.DeviceIdType.MESH
        )
    )
    pl.semaphore_wait(barrier, replicas - 1)

    def all_sum(phase, source, parts, result):
        def scatter(offset):
            other = peer(offset)
            return pltpu.make_async_remote_copy(
                src_ref=source.at[:, columns(other)],
                dst_ref=parts.at[offset],
                send_sem=send_sems.at[2 * phase, offset],
                recv_sem=recv_sems.at[2 * phase, offset],
                device_id={"dp": other},
                device_id_type=pl.DeviceIdType.MESH,
            )

        def spread(offset, owner):
            return pltpu.make_async_remote_copy(
                src_ref=result.at[:, columns(owner)],
                dst_ref=result.at[:, columns(owner)],
                send_sem=send_sems.at[2 * phase + 1, offset],
                recv_sem=recv_sems.at[2 * phase + 1, offset],
                device_id={"dp": peer(offset)},
                device_id_type=pl.DeviceIdType.MESH,
            )

        each(lambda offset: scatter(offset).start())

        def collect(offset, total):
            scatter(offset).wait_recv()
            return total + parts[offset]

        total = lax.fori_loop(1, replicas, collect, source[:, columns(me)])
        result[:, columns(me)] = total * share
        each(lambda offset: spread(offset, me).start())
        each(lambda offset: spread(offset, lax.rem(me - offset + replicas, replicas)).wait_recv())
        each(lambda offset: scatter(offset).wait_send())
        each(lambda offset: spread(offset, me).wait_send())

    all_sum(0, start_ref, parts_one, summed)
    mean_ref[...] = summed[:, 3328:4096]
    bases = []
    for start, size in ((0, 1024), (1024, 1024), (2048, 512), (2560, 512), (3072, 256)):
        basis = orthonormal_rows(summed[:, start : start + size])
        left_ref[:, start : start + size] = basis
        bases.append(basis)
    height = embed.shape[1]
    total = None
    for group in range(embed.shape[0]):
        term = right_product(bases[0][:, group * height : (group + 1) * height], embed[group])
        total = term if total is None else total + term
    partial[:, 0:512] = total
    partial[:, 512:1024] = right_product(bases[1], outer[...])
    for kind in range(3):
        partial[:, 1024 + kind * 256 : 1280 + kind * 256] = right_product(bases[2], attend[kind])
    partial[:, 1792:2816] = right_product(bases[3], inner[...])
    partial[:, 2816:3328] = right_product(bases[4], mixer[...])
    partial[:, 3328:] = jnp.zeros((8, partial.shape[1] - 3328), f32)
    all_sum(1, partial, parts_two, gathered)
    right_ref[...] = gathered[:, :3328]


def renew_all(
    step_rate, mixer_rate, left, right, mean, *refs,
):
    matrices, weights, moments = refs[0:5], refs[5:10], refs[10:15]
    vectors, vector_moments = refs[15:20], refs[20:25]
    errors, new_weights, new_moments = refs[25:30], refs[30:35], refs[35:40]
    new_vectors, new_vector_moments = refs[40:45], refs[45:50]
    lefts, rights = refs[50:55], refs[55:60]
    step = pl.program_id(0)

    def approx(basis, factor):
        left_high, left_low = split_two(basis)
        right_high, right_low = split_two(factor)
        return dot_tn(
            jnp.concatenate([left_high, left_low, left_high, left_low], axis=0),
            jnp.concatenate([right_high, right_high, right_low, right_low], axis=0),
        )

    def write(index, where, update, rate):
        errors[index][where] = matrices[index][where] - update
        moment = momentum_decay * moments[index][where] + update
        new_moments[index][where] = moment
        new_weights[index][where] = weights[index][where] - rate * moment

    def cut(start, size):
        return pl.ds(pl.multiple_of(start + step * size, 128), size)

    every = (slice(None), slice(None))
    groups, height, block = matrices[0].shape
    factor = right[:, cut(0, block)]
    for group in range(groups):
        write(
            0, (group, slice(None), slice(None)),
            approx(left[:, group * height : (group + 1) * height], factor), step_rate,
        )
    write(1, every, approx(left[:, cut(1024, matrices[1].shape[0])], right[:, 512:1024]), step_rate)
    basis = left[:, cut(2048, matrices[2].shape[1])]
    for kind in range(3):
        write(
            2, (kind, slice(None), slice(None)),
            approx(basis, right[:, 1024 + kind * 256 : 1280 + kind * 256]), step_rate,
        )
    write(3, every, approx(left[:, cut(2560, matrices[3].shape[0])], right[:, 1792:2816]), step_rate)
    write(4, every, approx(left[:, 3072:3328], right[:, cut(2816, matrices[4].shape[1])]), mixer_rate)

    @pl.when(step == 0)
    def _():
        for group in range(groups):
            lefts[0][group] = left[:, group * height : (group + 1) * height]
        lefts[1][...] = left[:, 1024:2048]
        lefts[2][...] = left[:, 2048:2560]
        lefts[3][...] = left[:, 2560:3072]
        lefts[4][...] = left[:, 3072:3328]
        rights[0][...] = right[:, 0:512]
        rights[1][...] = right[:, 512:1024]
        for kind in range(3):
            rights[2][kind] = right[:, 1024 + kind * 256 : 1280 + kind * 256]
        rights[3][...] = right[:, 1792:2816]
        rights[4][...] = right[:, 2816:3328]

        def renew(index, rows, columns, gradient):
            moment = momentum_decay * vector_moments[index][rows, columns] + gradient
            new_vector_moments[index][rows, columns] = moment
            new_vectors[index][rows, columns] = vectors[index][rows, columns] - step_rate * moment

        renew(0, slice(0, 3), slice(None), mean[0:3, :512])
        renew(1, slice(0, 2), slice(None), mean[3:5, :512])
        renew(2, slice(0, 3), slice(None), mean[5:8, :512])
        renew(2, slice(3, 4), slice(0, 256), mean[0:1, 512:])
        renew(2, slice(3, 4), slice(256, 512), mean[1:2, 512:])
        renew(3, slice(0, 1), slice(None), mean[2:3, 512:])
        renew(3, slice(1, 2), slice(None), mean[3:4, 512:])
        for index in range(4):
            renew(
                4, slice(0, 1), slice(index * 256, (index + 1) * 256),
                mean[4 + index : 5 + index, 512:],
            )


def call(kernel, outs, args, *, in_specs=None, scratch=(), limit=32, name=None):
    return pl.pallas_call(
        kernel,
        out_shape=outs,
        in_specs=in_specs if in_specs is not None else [VM] * len(args),
        out_specs=jax.tree.map(lambda _: VM, outs),
        scratch_shapes=list(scratch),
        compiler_params=pltpu.CompilerParams(vmem_limit_bytes=limit * MIB),
        name=name,
    )(*args)


def sds(shape, dtype=f32):
    return jax.ShapeDtypeStruct(shape, dtype)


def local(
    series, groups, counts, cotangent,
    embed_weight, embed_moment, embed_error, embed_start,
    attend_weight, attend_moment, attend_error, attend_start,
    mixer_weight, mixer_moment, mixer_error, mixer_start,
    inner_weight, inner_moment, inner_error, inner_start,
    outer_weight, outer_moment, outer_error, outer_start,
    embed_bias, embed_bias_moment, query_bias, query_bias_moment,
    inner_bias, inner_bias_moment, norm_gains, gains_moment, shared_biases, biases_moment,
):
    replicas = lax.axis_size("dp")
    half, windows, history = series.shape
    rows = 2 * half
    group_count, _, width = embed_weight.shape
    part = attend_weight.shape[2]
    inner_part = inner_weight.shape[1]
    units = 2 * inner_part
    turned = lambda a: a.transpose(1, 0, 2)

    def swap(values):
        return lax.ppermute(values, "mp", [(0, 1), (1, 0)])

    low = sds((rows, width), bf16)
    full = sds((rows, width))
    near = sds((half, width))
    send_one, series_own, table, bias_row, small = call(
        prepare_attention,
        [sds((half + 3 * part, width), bf16), sds((half, history), bf16), sds((history, width), bf16),
         sds((1, width)), sds((8, inner_part))],
        (groups, series, turned(attend_weight), embed_weight, embed_bias, query_bias, inner_bias[None]),
        in_specs=[SM] + [VM] * 6, limit=LIMITS[0],
        name="prepare_attention",
    )
    other_one = swap(send_one)
    small_other = swap(small)
    send_two, cot_own = call(
        prepare_feed,
        [sds((part + 2 * inner_part + half, width), bf16), sds((half, width), bf16)],
        (cotangent, mixer_weight, inner_weight, outer_weight), limit=LIMITS[1],
        name="prepare_feed",
    )
    other_two = swap(send_two)
    hidden, tokens, queries, keys, values, context, lse = call(
        attend_forward,
        [full, low, low, low, low, low, sds((rows, 128))],
        (counts, series_own, table, bias_row, send_one, other_one, small, small_other),
        in_specs=[SM] + [VM] * 7, limit=LIMITS[2],
        name="attend_forward",
    )
    (
        output_near, output_send, active, preact_grad, normed_low, feed_grad, attend_out, resid_one,
        context_grad, delta, sums, inner_sums, grads_send,
    ) = call(
        functools.partial(feed_forward, TILES),
        [near, near, sds((rows, units), bf16), sds((rows, units), bf16), low, low, low, full, low,
         sds((rows, 128), bf16), sds((8, width)), sds((8, units)),
         sds((2 * inner_part + part, width), bf16)],
        (counts, context, hidden, send_two, other_two, small, small_other, norm_gains, shared_biases, cot_own),
        in_specs=[SM] + [VM] * 9, limit=LIMITS[3],
        scratch=[pltpu.VMEM((rows // TILES, units), bf16)],
        name="feed_forward",
    )
    output_other = swap(output_send)
    grads_other = swap(grads_send)
    attend_near, send_three, series_near, series_far, sums_near, sums_far = call(
        attend_backward,
        [sds((3, width, part)), sds((3 * part + history, width), bf16), sds((half, history)),
         sds((half, history)), sds((16, width)), sds((16, width))],
        (groups, counts, queries, keys, values, lse, context_grad, delta, tokens, resid_one, send_one,
         other_one, table, series_own, sums, inner_sums),
        in_specs=[SM] * 2 + [VM] * 14, limit=LIMITS[4],
        scratch=[pltpu.VMEM((rows, width), bf16)] * 3,
        name="attend_backward",
    )
    other_three = swap(send_three)
    series_other = swap(series_far)
    sums_other = swap(sums_far)
    outer_matrix, inner_matrix, mixer_matrix, left_part, output = call(
        feed_matrices,
        [sds(outer_weight.shape), sds(inner_weight.shape), sds(mixer_weight.shape), sds((8, 1792)),
         sds((half, windows, width))],
        (active, preact_grad, normed_low, feed_grad, context, attend_out, grads_other,
         outer_error[0], inner_error[0], mixer_error[0], outer_start[0].T, inner_start.T, mixer_start[0].T,
         output_near, output_other),
        limit=LIMITS[5],
        name="feed_matrices",
    )
    attend_matrix, embed_matrix, left_partial, series_grad = call(
        other_matrices,
        [sds((3, width, part)), sds(embed_weight.shape), sds((8, 4096)), sds((half, windows, history))],
        (groups, attend_near, send_three, other_three, turned(attend_error[0]), embed_error[0],
         attend_start.transpose(0, 2, 1), embed_start.T, left_part, sums_near, sums_other,
         series_near, series_other),
        in_specs=[SM] + [VM] * 12, limit=LIMITS[6],
        name="other_matrices",
    )
    matrices = (embed_matrix, outer_matrix, attend_matrix, inner_matrix, mixer_matrix)
    padded = max(128, -(-4096 // replicas // 128) * 128)
    total = padded * replicas
    if total > 4096:
        left_partial = jnp.pad(left_partial, ((0, 0), (0, total - 4096)))
    left, right, mean = pl.pallas_call(
        functools.partial(reduce_factors, replicas),
        out_shape=[sds((8, 3328)), sds((8, 3328)), sds((8, 768))],
        in_specs=[VM] * 6,
        out_specs=[VM] * 3,
        scratch_shapes=[
            pltpu.VMEM((8, total), f32), pltpu.VMEM((8, total), f32), pltpu.VMEM((8, total), f32),
            pltpu.VMEM((replicas, 8, padded), f32), pltpu.VMEM((replicas, 8, padded), f32),
            pltpu.SemaphoreType.DMA((4, replicas)), pltpu.SemaphoreType.DMA((4, replicas)),
        ],
        compiler_params=pltpu.CompilerParams(
            collective_id=1, has_side_effects=True, vmem_limit_bytes=LIMITS[7] * MIB
        ),
        name="reduce_factors",
    )(left_partial, *matrices)

    step_rate = base_rate * math.sqrt(replicas * 7 / (windows * rows))
    mixer_rate = step_rate * math.sqrt(width / max(width * 16 // rows, 1))
    steps = 4
    whole = lambda a: pl.BlockSpec(a.shape, lambda i: (0,) * len(a.shape))
    column = lambda a: pl.BlockSpec((a.shape[0], a.shape[1] // steps), lambda i: (0, i))
    row = lambda a: pl.BlockSpec((a.shape[0] // steps, a.shape[1]), lambda i: (i, 0))
    middle = lambda a: pl.BlockSpec((a.shape[0], a.shape[1] // steps, a.shape[2]), lambda i: (0, i, 0))
    last = lambda a: pl.BlockSpec((a.shape[0], a.shape[1], a.shape[2] // steps), lambda i: (0, 0, i))
    specs = [spec(a) for spec, a in zip((last, row, middle, row, column), matrices)]
    vectors = (embed_bias, norm_gains, shared_biases, query_bias, inner_bias[None])
    vector_moments = (
        embed_bias_moment, gains_moment, biases_moment, query_bias_moment, inner_bias_moment[None]
    )
    vector_specs = [whole(a) for a in vectors]
    factors = [
        sds((group_count, 8, history)), sds((8, 1024)), sds((8, 512)), sds((8, 512)), sds((8, 256)),
        sds((8, 512)), sds((8, 512)), sds((3, 8, part)), sds((8, 1024)), sds((8, 512)),
    ]
    found = pl.pallas_call(
        functools.partial(renew_all, step_rate, mixer_rate),
        grid=(steps,),
        out_shape=[sds(a.shape) for a in matrices] * 3 + [sds(a.shape) for a in vectors] * 2 + factors,
        in_specs=[whole(left), whole(right), whole(mean)] + specs * 3 + vector_specs * 2,
        out_specs=specs * 3 + vector_specs * 2 + [whole(a) for a in factors],
        compiler_params=pltpu.CompilerParams(vmem_limit_bytes=LIMITS[8] * MIB),
        name="renew_all",
    )(
        left, right, mean, *matrices,
        embed_weight, outer_weight, turned(attend_weight), inner_weight, mixer_weight,
        embed_moment, outer_moment, turned(attend_moment), inner_moment, mixer_moment,
        *vectors, *vector_moments,
    )
    errors, weights, moments = found[0:5], found[5:10], found[10:15]
    new_vectors, new_vector_moments = found[15:20], found[20:25]
    lefts, rights = found[25:30], found[30:35]
    return (
        output,
        series_grad,
        weights[0],
        moments[0],
        errors[0][None],
        lefts[0].transpose(0, 2, 1),
        rights[0].T,
        turned(weights[2]),
        turned(moments[2]),
        turned(errors[2])[None],
        lefts[2].T[None],
        rights[2].transpose(0, 2, 1),
        weights[4],
        moments[4],
        errors[4][None],
        lefts[4].T,
        rights[4].T[None],
        weights[3],
        moments[3],
        errors[3][None],
        lefts[3].T[None],
        rights[3].T,
        weights[1],
        moments[1],
        errors[1][None],
        lefts[1].T,
        rights[1].T[None],
        new_vector_moments[0],
        new_vectors[0],
        new_vector_moments[3],
        new_vectors[3],
        new_vector_moments[4][0],
        new_vectors[4][0],
        new_vector_moments[1],
        new_vectors[1],
        new_vector_moments[2],
        new_vectors[2],
    )


def solution(mesh):
    return jax.shard_map(
        local,
        mesh=mesh,
        in_specs=(
            P("mp", "dp", None),
            P("dp"),
            P("dp"),
            P("mp", "dp", None),
            P(),
            P(),
            P("dp", None, None, None),
            P(),
            P(None, None, "mp"),
            P(None, None, "mp"),
            P("dp", None, None, "mp"),
            P(None, "mp", None),
            P("mp", None),
            P("mp", None),
            P("dp", "mp", None),
            P("mp", None, None),
            P(None, "mp"),
            P(None, "mp"),
            P("dp", None, "mp"),
            P("mp", None),
            P("mp", None),
            P("mp", None),
            P("dp", "mp", None),
            P("mp", None, None),
            P(),
            P(),
            P(None, "mp"),
            P(None, "mp"),
            P("mp"),
            P("mp"),
            P(),
            P(),
            P(),
            P(),
        ),
        out_specs=(
            P("mp", "dp", None),
            P("mp", "dp", None),
            P(),
            P(),
            P("dp", None, None, None),
            P(),
            P(),
            P(None, None, "mp"),
            P(None, None, "mp"),
            P("dp", None, None, "mp"),
            P("mp", None, None),
            P(None, "mp", None),
            P("mp", None),
            P("mp", None),
            P("dp", "mp", None),
            P("mp", None),
            P("mp", None, None),
            P(None, "mp"),
            P(None, "mp"),
            P("dp", None, "mp"),
            P("mp", None, None),
            P("mp", None),
            P("mp", None),
            P("mp", None),
            P("dp", "mp", None),
            P("mp", None),
            P("mp", None, None),
            P(),
            P(),
            P(None, "mp"),
            P(None, "mp"),
            P("mp"),
            P("mp"),
            P(),
            P(),
            P(),
            P(),
        ),
        check_vma=False,
    )
```

profile of v0, /device:TPU:0, one launch (start us, length us, event | category | flops | bytes accessed | tf_op | source)
XLA Modules:
  0.0 171.1 jit_solution(5323872783367932885)
XLA Ops:
  0.7 1.6 copy-done
  2.3 1.6 copy-done.1
  3.9 1.0 copy-done.13
  4.9 1.2 copy-done.18
  6.1 2.1 %prepare_feed.1 = (bf16[2752,512]{1,0:T(8,128)(2,1)S(1)}, bf16[448,512]{1,0:T(8,128)(2,1)S(1)}) custom-call(bf16[448,2,512]{2,1,0:T(2,128)(2,1)S(1)} %copy-done.18, f32[256,512]{1,0:T(8,128)S(1)} %copy-done.13, f32[512,1024]{1,0:T(8,128)S(1)} %copy-done, f32[1024,512]{1,0:T(8,128)S(1)} %copy-done.1), custom_call_target="tpu_custom_call" | custom-call | tf_op jit(solution)/shard_map/prepare_feed/pallas_call | solution.py:704
  8.9 2.5 %prepare_attention.1 = (bf16[1216,512]{1,0:T(8,128)(2,1)S(1)}, bf16[448,336]{1,0:T(8,128)(2,1)S(1)}, bf16[336,512]{1,0:T(8,128)(2,1)S(1)}, f32[1,512]{1,0:T(1,128)S(1)}, f32[8,1024]{1,0:T(8,128)S(1)}) custom-call(s32[2]{0:T(128)S(1)} %copy-done.52, bf16[448,2,336]{2,1,0:T(2,128)(2,1)S(1)} %copy-done.34, f32[3,512,256]{2,1,0:T(8,128)S(1)} %bitcast.50, ...), custom_call_target="tpu_custom_call" | custom-call | tf_op jit(solution)/shard_map/prepare_attention/pallas_call | solution.py:704
  11.9 3.5 %collective-permute-done.1.small_other = f32[8,1024]{1,0:T(8,128)S(1)} collective-permute-done((f32[8,1024]{1,0:T(8,128)S(1)}, f32[8,1024]{1,0:T(8,128)S(1)}, u32[]{:S(2)}, u32[]{:S(2)}) %collective-permute-start.1) | collective-permute-done | bytes 32800 | tf_op jit(solution)/shard_map/ppermute | solution.py:739
  15.5 15.3 %attend_forward.1 = (f32[896,512]{1,0:T(8,128)S(1)}, bf16[896,512]{1,0:T(8,128)(2,1)S(1)}, bf16[896,512]{1,0:T(8,128)(2,1)S(1)}, bf16[896,512]{1,0:T(8,128)(2,1)...) custom-call(s32[2]{0:T(128)S(1)} %copy-done.51, ...), custom_call_target="tpu_custom_call" | custom-call | tf_op jit(solution)/shard_map/attend_forward/pallas_call | solution.py:704
  31.7 1.2 copy-done.15
  32.9 0.9 copy-done.25
  37.4 1.7 copy-done.55
  39.1 26.8 %feed_forward.1 = (f32[448,512]{1,0:T(8,128)S(1)}, f32[448,512]{1,0:T(8,128)S(1)}, bf16[896,2048]{1,0:T(8,128)(2,1)}, bf16[896,2048]{1,0:T(8,128)(2,1)}, bf16[89...) custom-call(s32[2]{0:T(128)S(1)} %copy-done.51, ...), custom_call_target="tpu_custom_call" | custom-call | tf_op jit(solution)/shard_map/feed_forward/pallas_call | solution.py:704
  70.0 1.5 copy-done.16
  71.5 1.2 copy-done.32
  72.6 1.2 copy-done.33
  73.8 1.0 copy-done.37
  74.9 24.2 %attend_backward.1 = (f32[3,512,256]{2,1,0:T(8,128)S(1)}, bf16[1104,512]{1,0:T(8,128)(2,1)}, f32[448,336]{1,0:T(8,128)S(1)}, f32[448,336]{1,0:T(8,128)}, f32[16,512]{1,0:T(8,128)S(1)}, /*index=5*/f32[16,512]{1,0:T(8,128)S(1)}) custom-call(s32[2]{0:T(128)S(1)} %copy-done.52, s32[2]{0:T(128)S(1)} %copy-done.51, bf16[896,512]{1,0:T(8,128)(2,1)S(1)} %copy-done.28, ...), custom_call_target="tpu_custom_call" | custom-call | tf_op jit(solution)/shard_map/attend_backward/pallas_call | solution.py:704
  100.1 4.0 %collective-permute-done.4.output_far = f32[448,512]{1,0:T(8,128)S(1)} collective-permute-done((f32[448,512]{1,0:T(8,128)S(1)}, f32[448,512]{1,0:T(8,128)S(1)}, u32[]{:S(2)}, u32[]{:S(2)}) %collective-permute-start.4) | collective-permute-done | bytes 917536 | tf_op jit(solution)/shard_map/ppermute | solution.py:739
  104.3 1.2 copy-done.24
  105.4 1.0 copy-done.35
  106.5 9.8 %feed_matrices.1 = (f32[1024,512]{1,0:T(8,128)S(1)}, f32[512,1024]{1,0:T(8,128)S(1)}, f32[256,512]{1,0:T(8,128)S(1)}, f32[8,1792]{1,0:T(8,128)S(1)}, f32[448,2,512]{2,1,0:T(2,128)}) custom-call(bf16[896,2048]{1,0:T(8,128)(2,1)} %get-tuple-element.126.active_ref, bf16[896,2048]{1,0:T(8,128)(2,1)} %get-tuple-element.127.preact_ref, ...), custom_call_target="tpu_custom_call" | custom-call | tf_op jit(solution)/shard_map/feed_matrices/pallas_call | solution.py:704
  116.4 5.0 %other_matrices.1 = (f32[3,512,256]{2,1,0:T(8,128)S(1)}, f32[3,336,512]{2,1,0:T(8,128)S(1)}, f32[8,4096]{1,0:T(8,128)S(1)}, f32[448,2,336]{2,1,0:T(2,128)}) custom-call(s32[2]{0:T(128)S(1)} %copy-done.52, f32[3,512,256]{2,1,0:T(8,128)S(1)} %get-tuple-element.145.near_attend, bf16[1104,512]{1,0:T(8,128)(2,1)} %get-tuple-element.146.own, ...), custom_call_target="tpu_custom_call" | custom-call | tf_op jit(solution)/shard_map/other_matrices/pallas_call | solution.py:704
  121.4 31.0 %reduce_factors.1 = (f32[8,3328]{1,0:T(8,128)S(1)}, f32[8,3328]{1,0:T(8,128)S(1)}, f32[8,768]{1,0:T(8,128)S(1)}) custom-call(f32[8,4096]{1,0:T(8,128)S(1)} %get-tuple-element.153.start_ref, f32[3,336,512]{2,1,0:T(8,128)S(1)} %get-tuple-element.154.embed.refs_0_, f32[1024,512]{1,0:T(8,128)S(1)} %get-tuple-element.155.outer.refs_1_, ...), custom_call_target="tpu_custom_call" | custom-call | tf_op jit(solution)/shard_map/reduce_factors/pallas_call | solution.py:820
  154.3 16.6 %renew_all.1 = (f32[3,336,512]{2,1,0:T(8,128)}, f32[1024,512]{1,0:T(8,128)}, f32[3,512,256]{2,1,0:T(8,128)}, f32[512,1024]{1,0:T(8,128)}, f32[256,512]{1,0:T(8,1...) custom-call(f32[8,3328]{1,0:T(8,128)} %copy-done.38, ...), custom_call_target="tpu_custom_call" | custom-call | tf_op jit(solution)/shard_map/renew_all/pallas_call | solution.py:854
  (113 shorter events, 12.7 us)
Async XLA Ops:
  8.3 29.1 %collective-permute-start.2 = (bf16[2752,512]{1,0:T(8,128)(2,1)S(1)}, bf16[2752,512]{1,0:T(8,128)(2,1)S(1)}, u32[]{:S(2)}, u32[]{:S(2)}) collective-permute-start(bf16[2752,512]{1,0:T(8,128)(2,1)S(1)} %get-tuple-element.124.own), channel_id=1, source_target_pairs={{0,1},{1,0},{2,3},{3,2},{4,5},{5,4},{6,7},{7,6},{8,9},{9,8},{10,11... | collective-permute-start | bytes 8454152 | tf_op jit(solution)/shard_map/ppermute | solution.py:739
  11.3 27.7 %copy-start.42 = (f32[4,512]{1,0:T(4,128)S(1)}, f32[4,512]{1,0:T(4,128)}, u32[]{:S(2)}) copy-start(f32[4,512]{1,0:T(4,128)} %refs_17_.1) | copy-start | bytes 24580
  11.3 27.7 %copy-start.48 = (f32[2,512]{1,0:T(2,128)S(1)}, f32[2,512]{1,0:T(2,128)}, u32[]{:S(2)}) copy-start(f32[2,512]{1,0:T(2,128)} %refs_16_.1) | copy-start | bytes 12292
  11.3 4.1 %collective-permute-start = (bf16[1216,512]{1,0:T(8,128)(2,1)S(1)}, bf16[1216,512]{1,0:T(8,128)(2,1)S(1)}, u32[]{:S(2)}, u32[]{:S(2)}) collective-permute-start(bf16[1216,512]{1,0:T(8,128)(2,1)S(1)} %get-tuple-element.120.own), channel_id=1, source_target_pairs={{0,1},{1,0},{2,3},{3,2},{4,5},{5,4},{6,7},{7,6},{8,9},{9,8},{10,11... | collective-permute-start | bytes 3735560 | tf_op jit(solution)/shard_map/ppermute | solution.py:739
  11.5 4.0 %collective-permute-start.1 = (f32[8,1024]{1,0:T(8,128)S(1)}, f32[8,1024]{1,0:T(8,128)S(1)}, u32[]{:S(2)}, u32[]{:S(2)}) collective-permute-start(f32[8,1024]{1,0:T(8,128)S(1)} %get-tuple-element.121.small), channel_id=1, source_target_pairs={{0,1},{1,0},{2,3},{3,2},{4,5},{5,4},{6,7},{7,6},{8,9},{9,8},{10,11... | collective-permute-start | bytes 98312 | tf_op jit(solution)/shard_map/ppermute | solution.py:739
  39.0 30.9 %copy-start.26 = (bf16[896,512]{1,0:T(8,128)(2,1)S(1)}, bf16[896,512]{1,0:T(8,128)(2,1)}, u32[]{:S(2)}) copy-start(bf16[896,512]{1,0:T(8,128)(2,1)} %copy-done.25) | copy-start | bytes 2752516
  39.0 30.9 %copy-start.28 = (bf16[896,512]{1,0:T(8,128)(2,1)S(1)}, bf16[896,512]{1,0:T(8,128)(2,1)}, u32[]{:S(2)}) copy-start(bf16[896,512]{1,0:T(8,128)(2,1)} %copy-done.27) | copy-start | bytes 2752516
  39.0 30.9 %copy-start.30 = (bf16[896,512]{1,0:T(8,128)(2,1)S(1)}, bf16[896,512]{1,0:T(8,128)(2,1)}, u32[]{:S(2)}) copy-start(bf16[896,512]{1,0:T(8,128)(2,1)} %copy-done.29) | copy-start | bytes 2752516
  69.6 34.6 %collective-permute-start.3 = (bf16[2304,512]{1,0:T(8,128)(2,1)}, bf16[2304,512]{1,0:T(8,128)(2,1)}, u32[]{:S(2)}, u32[]{:S(2)}) collective-permute-start(bf16[2304,512]{1,0:T(8,128)(2,1)} %get-tuple-element.131), channel_id=1, source_target_pairs={{0,1},{1,0},{2,3},{3,2},{4,5},{5,4},{6,7},{7,6},{8,9},{9,8},{10,11... | collective-permute-start | bytes 7077896 | tf_op jit(solution)/shard_map/ppermute | solution.py:739
  74.8 24.4 %copy-start.54 = (f32[448,512]{1,0:T(8,128)S(1)}, f32[448,512]{1,0:T(8,128)}, u32[]{:S(2)}) copy-start(f32[448,512]{1,0:T(8,128)} %copy-done.53) | copy-start | bytes 2752516
  74.8 29.4 %copy-start.9 = (bf16[896,512]{1,0:T(8,128)(2,1)S(1)}, bf16[896,512]{1,0:T(8,128)(2,1)}, u32[]{:S(2)}) copy-start(bf16[896,512]{1,0:T(8,128)(2,1)} %copy-done.8) | copy-start | bytes 2752516
  74.8 29.4 %copy-start.11 = (f32[1,1024,512]{2,1,0:T(8,128)S(1)}, f32[1,1024,512]{2,1,0:T(8,128)}, u32[]{:S(2)}) copy-start(f32[1,1024,512]{2,1,0:T(8,128)} %param.56) | copy-start | bytes 6291460
  74.8 29.4 %copy-start.20 = (bf16[896,512]{1,0:T(8,128)(2,1)S(1)}, bf16[896,512]{1,0:T(8,128)(2,1)}, u32[]{:S(2)}) copy-start(bf16[896,512]{1,0:T(8,128)(2,1)} %copy-done.19) | copy-start | bytes 2752516
  74.8 29.4 %copy-start.22 = (bf16[896,512]{1,0:T(8,128)(2,1)S(1)}, bf16[896,512]{1,0:T(8,128)(2,1)}, u32[]{:S(2)}) copy-start(bf16[896,512]{1,0:T(8,128)(2,1)} %copy-done.21) | copy-start | bytes 2752516
  74.8 29.4 %copy-start.40 = (f32[1024,8]{0,1:T(8,128)S(1)}, f32[1024,8]{0,1:T(8,128)}, u32[]{:S(2)}) copy-start(f32[1024,8]{0,1:T(8,128)} %param.53) | copy-start | bytes 98308
  74.9 29.4 %copy-start.45 = (f32[1,512,8]{1,2,0:T(8,128)S(1)}, f32[1,512,8]{1,2,0:T(8,128)}, u32[]{:S(2)}) copy-start(f32[1,512,8]{1,2,0:T(8,128)} %param.57) | copy-start | bytes 49156
  74.9 29.4 %copy-start.46 = (f32[1,512,8]{1,2,0:T(8,128)S(1)}, f32[1,512,8]{1,2,0:T(8,128)}, u32[]{:S(2)}) copy-start(f32[1,512,8]{1,2,0:T(8,128)} %param.49) | copy-start | bytes 49156
  99.1 17.2 %collective-permute-start.5 = (bf16[1104,512]{1,0:T(8,128)(2,1)}, bf16[1104,512]{1,0:T(8,128)(2,1)S(1)}, u32[]{:S(2)}, u32[]{:S(2)}) collective-permute-start(bf16[1104,512]{1,0:T(8,128)(2,1)} %get-tuple-element.146.own), channel_id=1, source_target_pairs={{0,1},{1,0},{2,3},{3,2},{4,5},{5,4},{6,7},{7,6},{8,9},{9,8},{10,11... | collective-permute-start | bytes 3391496 | tf_op jit(solution)/shard_map/ppermute | solution.py:739
  99.2 4.9 %collective-permute-start.4 = (f32[448,512]{1,0:T(8,128)S(1)}, f32[448,512]{1,0:T(8,128)S(1)}, u32[]{:S(2)}, u32[]{:S(2)}) collective-permute-start(f32[448,512]{1,0:T(8,128)S(1)} %copy-done.54), channel_id=1, source_target_pairs={{0,1},{1,0},{2,3},{3,2},{4,5},{5,4},{6,7},{7,6},{8,9},{9,8},{10,11... | collective-permute-start | bytes 2752520 | tf_op jit(solution)/shard_map/ppermute | solution.py:739
  99.6 16.7 %collective-permute-start.7 = (f32[448,336]{1,0:T(8,128)}, f32[448,336]{1,0:T(8,128)S(1)}, u32[]{:S(2)}, u32[]{:S(2)}) collective-permute-start(f32[448,336]{1,0:T(8,128)} %get-tuple-element.151), channel_id=1, source_target_pairs={{0,1},{1,0},{2,3},{3,2},{4,5},{5,4},{6,7},{7,6},{8,9},{9,8},{10,11... | collective-permute-start | bytes 1806344 | tf_op jit(solution)/shard_map/ppermute | solution.py:739
  99.8 16.5 %collective-permute-start.6 = (f32[16,512]{1,0:T(8,128)S(1)}, f32[16,512]{1,0:T(8,128)S(1)}, u32[]{:S(2)}, u32[]{:S(2)}) collective-permute-start(f32[16,512]{1,0:T(8,128)S(1)} %get-tuple-element.149), channel_id=1, source_target_pairs={{0,1},{1,0},{2,3},{3,2},{4,5},{5,4},{6,7},{7,6},{8,9},{9,8},{10,11... | collective-permute-start | bytes 98312 | tf_op jit(solution)/shard_map/ppermute | solution.py:739
  106.5 9.9 %copy-start.47 = (f32[512,8]{0,1:T(8,128)S(1)}, f32[512,8]{0,1:T(8,128)}, u32[]{:S(2)}) copy-start(f32[512,8]{0,1:T(8,128)} %param.41) | copy-start | bytes 49156
  121.3 31.1 %copy-start.5 = (f32[3,336,512]{2,1,0:T(8,128)}, f32[3,336,512]{2,1,0:T(8,128)S(1)}, u32[]{:S(2)}) copy-start(f32[3,336,512]{2,1,0:T(8,128)S(1)} %get-tuple-element.154.embed.refs_0_) | copy-start | bytes 6193156
  121.3 31.1 %copy-start.7 = (f32[3,512,256]{2,1,0:T(8,128)}, f32[3,512,256]{2,1,0:T(8,128)S(1)}, u32[]{:S(2)}) copy-start(f32[3,512,256]{2,1,0:T(8,128)S(1)} %get-tuple-element.156.attend.refs_2_) | copy-start | bytes 4718596
  (40 other events, 99.8 us)
where the time goes:
time: 172 us; the launch traced here: 171 us
  Pallas kernels  133 us (77%)
  local copies, waits for them, and re-layouts  26.5 us (15%)
  waiting for transfers between devices  7.59 us (4%)
  starting transfers between devices  2.48 us (1%)
    pallas_call x7, Pallas kernels, call(): pl.pallas_call(kernel, out_shape=outs, in_specs=in_specs if in_specs is n...  85.7 us
    pallas_call x1, Pallas kernels, local(): pl.pallas_call(functools.partial(reduce_factors, replicas), out_shape=[sd...  31 us
    unnamed x112, local copies, waits for them, and re-layouts  26.5 us
    pallas_call x1, Pallas kernels, local(): pl.pallas_call(functools.partial(renew_all, step_rate, mixer_rate), grid=...  16.6 us
    ppermute x8, waiting for transfers between devices, swap(): return lax.ppermute(values, 'mp', [(0, 1), (1, 0)])  7.59 us
  transfers between devices with their start and end apart: 8, of which 2 were waited for; matrix products, arithmetic and copies ran while one was open for 0% of the time, Pallas kernels for 30%

commit v1 on v0

--- a/solution.py
+++ b/solution.py
@@ -20,7 +20,7 @@
 bf16 = jnp.bfloat16
 VMEM = pltpu.VMEM
 VM = pl.BlockSpec(memory_space=pltpu.VMEM)
-SM = pl.BlockSpec(memory_space=pltpu.SMEM)
+HB = pl.BlockSpec(memory_space=pltpu.HBM)
 MIB = 1024 * 1024
 
 
@@ -50,13 +50,8 @@
     return jnp.where(place == 0, high, jnp.where(place == 1, middle, last)).astype(bf16)
 
 
-LIMITS = (20, 24, 32, 48, 40, 40, 24, 20, 56)
+LIMITS = (12, 14, 12, 8, 16, 8, 8, 28)
 TILES = 4
-
-
-def place_and_count(counts):
-    position = lax.axis_index("mp")
-    return position, counts[position]
 
 
 def row_number(rows, position):
@@ -99,38 +94,104 @@
         pair_ref[:, 0, :] = theirs[...]
 
 
-def prepare_attention(
-    groups, series, attend, embed, embed_bias, query_bias, inner_bias,
-    send, series_own, table, bias_row, small,
+def three_parts(x):
+    high = x.astype(bf16)
+    rest = x - high.astype(f32)
+    middle = rest.astype(bf16)
+    return high, middle, (rest - middle.astype(f32)).astype(bf16)
+
+
+def prepare(
+    groups_hbm, counts_hbm, series_hbm, attend_hbm, query_bias_hbm, inner_bias_hbm,
+    cot_hbm, mixer_hbm, inner_hbm, outer_hbm,
+    send, received, series_own, small, facts, send_feed, cot_own,
+    groups, counts, series, attend, query_bias, inner_bias, cotangent, mixer, inner, outer,
+    done, send_sems, recv_sems,
 ):
+    position = lax.axis_index("mp")
+    partner = {"mp": 1 - position}
+    barrier = pltpu.get_barrier_semaphore()
+    pl.semaphore_signal(barrier, inc=1, device_id=partner, device_id_type=pl.DeviceIdType.MESH)
+    copies = []
+    for source, target in (
+        (query_bias_hbm, query_bias), (inner_bias_hbm, inner_bias), (attend_hbm, attend),
+        (series_hbm, series), (groups_hbm, groups), (counts_hbm, counts), (cot_hbm, cotangent),
+        (mixer_hbm, mixer), (inner_hbm, inner), (outer_hbm, outer),
+    ):
+        copies.append(pltpu.make_async_copy(source, target, done.at[len(copies)]))
+        copies[-1].start()
     half, _, history = series.shape
+    width = send.shape[1]
     depth = attend.shape[1] // 2
-    send[:half, 256:] = jnp.zeros((half, send.shape[1] - 256), bf16)
-    split_pair(series, series_own, send.at[:half], slice(0, history))
+    end = half + 3 * depth
+    part = query_bias.shape[1]
+    trades = [
+        pltpu.make_async_remote_copy(
+            src_ref=send.at[rows], dst_ref=received.at[rows], send_sem=send_sems.at[index],
+            recv_sem=recv_sems.at[index], device_id=partner, device_id_type=pl.DeviceIdType.MESH,
+        )
+        for index, rows in enumerate((slice(half, end + 16), slice(0, half)))
+    ]
+    copies[0].wait()
+    copies[1].wait()
+    small[...] = jnp.zeros_like(small)
+    small[0:2, :part] = query_bias[...]
+    small[2:3, :] = inner_bias[...]
+    values = jnp.concatenate(
+        [
+            jnp.concatenate([query_bias[0:1, :], query_bias[1:2, :]], axis=1),
+            inner_bias[:, :width],
+            inner_bias[:, width:],
+            jnp.zeros((1, width), f32),
+        ],
+        axis=0,
+    )
+    send[end : end + 16, :] = jnp.concatenate(
+        [*three_parts(values), jnp.zeros((4, width), bf16)], axis=0
+    )
+    copies[2].wait()
     for kind in range(3):
         rows = slice(half + kind * depth, half + (kind + 1) * depth)
         send[rows, :256] = attend[kind, :depth, :].astype(bf16)
         send[rows, 256:] = attend[kind, depth:, :].astype(bf16)
-    group = groups[lax.axis_index("mp")]
-    chosen = embed[group]
-    row = lax.broadcasted_iota(jnp.int32, chosen.shape, 0)
-    table[...] = jnp.where(row >= history - lookback_of(group, history), chosen, 0.0).astype(bf16)
-    row = lax.broadcasted_iota(jnp.int32, embed_bias.shape, 0)
-    bias_row[...] = jnp.sum(jnp.where(row == group, embed_bias[...], 0.0), axis=0, keepdims=True)
-    small[...] = jnp.zeros_like(small)
-    small[0:2, : query_bias.shape[1]] = query_bias[...]
-    small[2:3, :] = inner_bias[...]
-
-
-def prepare_feed(cotangent, mixer, inner, outer, send, cot_own):
-    half = cotangent.shape[0]
-    m, d = mixer.shape[0], inner.shape[0]
-    o = outer.shape[0]
-    send[:m] = mixer[...].astype(bf16)
-    send[m : m + d] = inner[:, :512].astype(bf16)
-    send[m + d : m + 2 * d] = inner[:, 512:].astype(bf16)
-    send[m + 2 * d : m + 2 * d + o] = outer[...].astype(bf16)
-    split_pair(cotangent, cot_own, send.at[m + 2 * d + o :], slice(None))
+    pl.semaphore_wait(barrier, 1)
+    trades[0].start()
+    send[:half, 256:] = jnp.zeros((half, width - 256), bf16)
+    copies[3].wait()
+    split_pair(series, series_own, send.at[:half], slice(0, history))
+    trades[1].start()
+    copies[4].wait()
+    copies[5].wait()
+    group = jnp.where(position == 0, groups[0], groups[1])
+    other_group = jnp.where(position == 0, groups[1], groups[0])
+    count = jnp.where(position == 0, counts[0], counts[1])
+    first = history - lookback_of(group, history)
+    row = lax.broadcasted_iota(jnp.int32, facts.shape, 0)
+    facts[...] = jnp.where(
+        row == 0, count, jnp.where(row == 1, first, jnp.where(row == 2, group, other_group))
+    )
+    m, d, o = mixer.shape[0], inner.shape[0], outer.shape[0]
+    copies[6].wait()
+    split_pair(cotangent, cot_own, send_feed.at[m + 2 * d + o :], slice(None))
+    copies[7].wait()
+    send_feed[:m] = mixer[...].astype(bf16)
+    copies[8].wait()
+    send_feed[m : m + d] = inner[:, :512].astype(bf16)
+    send_feed[m + d : m + 2 * d] = inner[:, 512:].astype(bf16)
+    copies[9].wait()
+    send_feed[m + 2 * d : m + 2 * d + o] = outer[...].astype(bf16)
+    for trade in trades:
+        trade.wait()
+
+
+def unpack_small(other, small_other):
+    part = other.shape[1] // 2
+    parts = other[other.shape[0] - 16 :, :].astype(f32)
+    values = parts[0:4] + parts[4:8] + parts[8:12]
+    small_other[0:1, :part] = values[0:1, :part]
+    small_other[1:2, :part] = values[0:1, part:]
+    small_other[2:3, : 2 * part] = values[1:2, :]
+    small_other[2:3, 2 * part :] = values[2:3, :]
 
 
 def attend_block(pack, half, kind):
@@ -139,16 +200,24 @@
 
 
 def attend_forward(
-    counts, series_own, table, embed_bias, own, other, small, small_other,
-    hidden_ref, token_ref, query_ref, key_ref, value_ref, context_ref, lse_ref,
+    facts, series_own, embed, embed_bias, own, other, small,
+    hidden_ref, token_ref, query_ref, key_ref, value_ref, context_ref, lse_ref, small_other, table,
 ):
+    unpack_small(other, small_other)
+    chosen, bias_row = embed[0], embed_bias[0:1, :]
+    for group in range(1, embed.shape[0]):
+        here = facts[2:3, 0:1] == group
+        chosen = jnp.where(here, embed[group], chosen)
+        bias_row = jnp.where(here, embed_bias[group : group + 1, :], bias_row)
+    row = lax.broadcasted_iota(jnp.int32, chosen.shape, 0)
+    table[...] = jnp.where(row >= facts[1:2, 0:1], chosen, 0.0).astype(bf16)
     rows, width = hidden_ref.shape
     half, history = series_own.shape
     part = width // 2
     head_dim = width // HEADS
-    position, count = place_and_count(counts)
+    position, count = lax.axis_index("mp"), facts[0:1, 0:1]
     for index, block in enumerate((series_own[...], other[:half, :history])):
-        values = dot_nn(block, table[...]) + embed_bias[...]
+        values = dot_nn(block, table[...]) + bias_row
         hidden_ref[pl.ds(index * half, half), :] = values
         token_ref[pl.ds(index * half, half), :] = values.astype(bf16)
     scale = head_dim**-0.5 * log2_e
@@ -211,7 +280,7 @@
 
 
 def feed_forward(
-    tiles, counts, context_ref, hidden_ref, own, other, small, small_other, gains, biases, cot_own,
+    tiles, facts, context_ref, hidden_ref, own, other, small, small_other, gains, biases, cot_own,
     output_ref, output_send, active_ref, preact_ref, normed_ref, feed_ref, attend_ref, resid_ref,
     context_grad_ref, delta_ref, sums_ref, inner_sum_ref, grads_send, slope_ref,
 ):
@@ -222,7 +291,7 @@
     units = active_ref.shape[1]
     inner_part = units // 2
     chunk = 512
-    position, count = place_and_count(counts)
+    position, count = lax.axis_index("mp"), facts[0:1, 0:1]
     sums_ref[...] = jnp.zeros_like(sums_ref)
     inner_sum_ref[...] = jnp.zeros_like(inner_sum_ref)
     at_inner = part
@@ -339,7 +408,7 @@
 
 
 def attend_backward(
-    groups, counts, query_ref, key_ref, value_ref, lse_ref, context_grad_ref, delta_ref,
+    facts, query_ref, key_ref, value_ref, lse_ref, context_grad_ref, delta_ref,
     token_ref, resid_ref, own, other, table, series_own, sums_ref, inner_sum_ref,
     attend_own, send, series_near, series_far, near_out, far_out,
     dquery_ref, dkey_ref, dvalue_ref,
@@ -348,7 +417,7 @@
     head_dim = width // HEADS
     half, history = series_own.shape
     part = width // 2
-    position, count = place_and_count(counts)
+    position, count = lax.axis_index("mp"), facts[0:1, 0:1]
     lane = lax.broadcasted_iota(jnp.int32, (rows, 128), 1)
     dead = row_number(rows, position) >= count
     extra_query = jnp.where(lane == 127, jnp.ones((rows, 128), bf16), three_way(-lse_ref[...], lane))
@@ -418,7 +487,7 @@
     series_far[...] = dot_nt(low[half:], table[...])
     table_grad = dot_tn(series_own[...], low[:half]) + dot_tn(other[:half, :history], low[half:])
     row = lax.broadcasted_iota(jnp.int32, table_grad.shape, 0)
-    seen = row >= history - lookback_of(groups[position], history)
+    seen = row >= facts[1:2, 0:1]
     send[3 * part :, :] = jnp.where(seen, table_grad, 0.0).astype(bf16)
     shared = sums_ref[0:7, :]
     bias_grad = jnp.sum(low.astype(f32), axis=0, keepdims=True)
@@ -481,44 +550,6 @@
     left[:, 1536:1792] = left_product(s_mixer[...], mixer[...])
 
 
-def other_matrices(
-    groups, near_attend, own, received, e_attend, e_embed, s_attend, s_embed, left_part, near, far,
-    series_near, series_far,
-    attend, embed, left, series_grad,
-):
-    part = near_attend.shape[2]
-    position = lax.axis_index("mp")
-    join_pair(series_near, series_far, series_grad)
-    total = None
-    for kind in range(3):
-        rows = slice(kind * part, (kind + 1) * part)
-        block = jnp.concatenate([received[rows, :part], received[rows, part:]], axis=0)
-        attend[kind] = near_attend[kind] + block.astype(f32) + e_attend[kind]
-        term = left_product(s_attend[kind], attend[kind])
-        total = term if total is None else total + term
-    mine, theirs = groups[position], groups[1 - position]
-    table_near = own[3 * part :, :].astype(f32)
-    table_far = received[3 * part :, :].astype(f32)
-    pieces = []
-    for group in range(embed.shape[0]):
-        grad = jnp.where(mine == group, table_near, 0.0) + jnp.where(theirs == group, table_far, 0.0)
-        embed[group] = grad + e_embed[group]
-        pieces.append(left_product(s_embed[...], embed[group]))
-    used = embed.shape[0] * embed.shape[1]
-    left[:, 0:1024] = jnp.concatenate(pieces + [jnp.zeros((8, 1024 - used), f32)], axis=1)
-    left[:, 1024:2048] = left_part[:, 0:1024]
-    left[:, 2048:2560] = total
-    left[:, 2560:3328] = left_part[:, 1024:1792]
-    common = near[1:7, :] + far[1:7, :]
-    row = lax.broadcasted_iota(jnp.int32, (3, near.shape[1]), 0)
-    bias = jnp.where(row == mine, near[0:1, :], 0.0) + jnp.where(row == theirs, far[0:1, :], 0.0)
-    left[:, 3328:3840] = jnp.concatenate([bias, common[:5]], axis=0)
-    rest = jnp.concatenate([common[5:6], near[7:10, :] + far[7:10, :]], axis=0)
-    for row in range(4):
-        left[2 * row : 2 * row + 1, 3840:4096] = rest[row : row + 1, :256]
-        left[2 * row + 1 : 2 * row + 2, 3840:4096] = rest[row : row + 1, 256:]
-
-
 def orthonormal_rows(vectors):
     rank = vectors.shape[0]
     row = lax.broadcasted_iota(jnp.int32, vectors.shape, 0)
@@ -534,9 +565,10 @@
 
 
 def reduce_factors(
-    replicas, start_ref, embed, outer, attend, inner, mixer,
-    left_ref, right_ref, mean_ref,
-    summed, partial, gathered, parts_one, parts_two, send_sems, recv_sems,
+    replicas, facts, near_attend, own, received, e_attend, e_embed, s_attend, s_embed, left_part,
+    near, far, outer, inner, mixer,
+    left_ref, right_ref, mean_ref, attend, embed,
+    start_ref, summed, partial, gathered, parts_one, parts_two, send_sems, recv_sems,
 ):
     me = lax.axis_index("dp")
     barrier = pltpu.get_barrier_semaphore()
@@ -561,6 +593,37 @@
             barrier, inc=1, device_id={"dp": peer(offset)}, device_id_type=pl.DeviceIdType.MESH
         )
     )
+    part = near_attend.shape[2]
+    total = None
+    for kind in range(3):
+        rows = slice(kind * part, (kind + 1) * part)
+        block = jnp.concatenate([received[rows, :part], received[rows, part:]], axis=0)
+        attend[kind] = near_attend[kind] + block.astype(f32) + e_attend[kind]
+        term = left_product(s_attend[kind], attend[kind])
+        total = term if total is None else total + term
+    mine, theirs = facts[2:3, 0:1], facts[3:4, 0:1]
+    table_near = own[3 * part :, :].astype(f32)
+    table_far = received[3 * part :, :].astype(f32)
+    pieces = []
+    for group in range(embed.shape[0]):
+        grad = jnp.where(mine == group, table_near, 0.0) + jnp.where(theirs == group, table_far, 0.0)
+        embed[group] = grad + e_embed[group]
+        pieces.append(left_product(s_embed[...], embed[group]))
+    used = embed.shape[0] * embed.shape[1]
+    start_ref[:, 0:1024] = jnp.concatenate(pieces + [jnp.zeros((8, 1024 - used), f32)], axis=1)
+    start_ref[:, 1024:2048] = left_part[:, 0:1024]
+    start_ref[:, 2048:2560] = total
+    start_ref[:, 2560:3328] = left_part[:, 1024:1792]
+    common = near[1:7, :] + far[1:7, :]
+    row = lax.broadcasted_iota(jnp.int32, (3, near.shape[1]), 0)
+    bias = jnp.where(row == mine, near[0:1, :], 0.0) + jnp.where(row == theirs, far[0:1, :], 0.0)
+    start_ref[:, 3328:3840] = jnp.concatenate([bias, common[:5]], axis=0)
+    rest = jnp.concatenate([common[5:6], near[7:10, :] + far[7:10, :]], axis=0)
+    for row in range(4):
+        start_ref[2 * row : 2 * row + 1, 3840:4096] = rest[row : row + 1, :256]
+        start_ref[2 * row + 1 : 2 * row + 2, 3840:4096] = rest[row : row + 1, 256:]
+    if start_ref.shape[1] > 4096:
+        start_ref[:, 4096:] = jnp.zeros((8, start_ref.shape[1] - 4096), f32)
     pl.semaphore_wait(barrier, replicas - 1)
 
     def all_sum(phase, source, parts, result):
@@ -622,14 +685,15 @@
 
 
 def renew_all(
-    step_rate, mixer_rate, left, right, mean, *refs,
+    step_rate, mixer_rate, left, right, mean, series_near, series_far, *refs,
 ):
     matrices, weights, moments = refs[0:5], refs[5:10], refs[10:15]
     vectors, vector_moments = refs[15:20], refs[20:25]
     errors, new_weights, new_moments = refs[25:30], refs[30:35], refs[35:40]
     new_vectors, new_vector_moments = refs[40:45], refs[45:50]
-    lefts, rights = refs[50:55], refs[55:60]
+    lefts, rights, series_grad = refs[50:55], refs[55:60], refs[60]
     step = pl.program_id(0)
+    join_pair(series_near, series_far, series_grad)
 
     def approx(basis, factor):
         left_high, left_low = split_two(basis)
@@ -700,7 +764,7 @@
             )
 
 
-def call(kernel, outs, args, *, in_specs=None, scratch=(), limit=32, name=None):
+def call(kernel, outs, args, *, cost, in_specs=None, scratch=(), limit=32, name=None):
     return pl.pallas_call(
         kernel,
         out_shape=outs,
@@ -708,8 +772,15 @@
         out_specs=jax.tree.map(lambda _: VM, outs),
         scratch_shapes=list(scratch),
         compiler_params=pltpu.CompilerParams(vmem_limit_bytes=limit * MIB),
+        cost_estimate=estimate(cost),
         name=name,
     )(*args)
+
+
+def estimate(microseconds):
+    return pl.CostEstimate(
+        flops=int(microseconds * 1e9), bytes_accessed=int(microseconds * 2e6), transcendentals=0
+    )
 
 
 def sds(shape, dtype=f32):
@@ -741,28 +812,43 @@
     low = sds((rows, width), bf16)
     full = sds((rows, width))
     near = sds((half, width))
-    send_one, series_own, table, bias_row, small = call(
-        prepare_attention,
-        [sds((half + 3 * part, width), bf16), sds((half, history), bf16), sds((history, width), bf16),
-         sds((1, width)), sds((8, inner_part))],
-        (groups, series, turned(attend_weight), embed_weight, embed_bias, query_bias, inner_bias[None]),
-        in_specs=[SM] + [VM] * 6, limit=LIMITS[0],
-        name="prepare_attention",
-    )
-    other_one = swap(send_one)
-    small_other = swap(small)
-    send_two, cot_own = call(
-        prepare_feed,
-        [sds((part + 2 * inner_part + half, width), bf16), sds((half, width), bf16)],
-        (cotangent, mixer_weight, inner_weight, outer_weight), limit=LIMITS[1],
-        name="prepare_feed",
+    packed = sds((half + 3 * part + 16, width), bf16)
+    send_one, other_one, series_own, small, facts, send_two, cot_own = pl.pallas_call(
+        prepare,
+        out_shape=[
+            packed, packed, sds((half, history), bf16), sds((8, inner_part)), sds((8, 128), jnp.int32),
+            sds((part + 2 * inner_part + half, width), bf16), sds((half, width), bf16),
+        ],
+        in_specs=[HB] * 10,
+        out_specs=[VM] * 7,
+        scratch_shapes=[
+            pltpu.SMEM(groups.shape, jnp.int32), pltpu.SMEM(counts.shape, jnp.int32),
+            pltpu.VMEM(series.shape, bf16), pltpu.VMEM((3, width, part), f32),
+            pltpu.VMEM(query_bias.shape, f32), pltpu.VMEM((1, inner_part), f32),
+            pltpu.VMEM(cotangent.shape, bf16), pltpu.VMEM(mixer_weight.shape, f32),
+            pltpu.VMEM(inner_weight.shape, f32), pltpu.VMEM(outer_weight.shape, f32),
+            pltpu.SemaphoreType.DMA((10,)), pltpu.SemaphoreType.DMA((2,)), pltpu.SemaphoreType.DMA((2,)),
+        ],
+        compiler_params=pltpu.CompilerParams(
+            collective_id=2, has_side_effects=True, vmem_limit_bytes=LIMITS[0] * MIB
+        ),
+        cost_estimate=estimate(7),
+        name="prepare",
+    )(
+        *(
+            pltpu.with_memory_space_constraint(a, pltpu.HBM)
+            for a in (
+                groups, counts, series, turned(attend_weight), query_bias, inner_bias[None],
+                cotangent, mixer_weight, inner_weight, outer_weight,
+            )
+        )
     )
     other_two = swap(send_two)
-    hidden, tokens, queries, keys, values, context, lse = call(
+    hidden, tokens, queries, keys, values, context, lse, small_other, table = call(
         attend_forward,
-        [full, low, low, low, low, low, sds((rows, 128))],
-        (counts, series_own, table, bias_row, send_one, other_one, small, small_other),
-        in_specs=[SM] + [VM] * 7, limit=LIMITS[2],
+        [full, low, low, low, low, low, sds((rows, 128)), sds((8, inner_part)), sds((history, width), bf16)],
+        (facts, series_own, embed_weight, embed_bias, send_one, other_one, small),
+        limit=LIMITS[2], cost=15,
         name="attend_forward",
     )
     (
@@ -773,8 +859,8 @@
         [near, near, sds((rows, units), bf16), sds((rows, units), bf16), low, low, low, full, low,
          sds((rows, 128), bf16), sds((8, width)), sds((8, units)),
          sds((2 * inner_part + part, width), bf16)],
-        (counts, context, hidden, send_two, other_two, small, small_other, norm_gains, shared_biases, cot_own),
-        in_specs=[SM] + [VM] * 9, limit=LIMITS[3],
+        (facts, context, hidden, send_two, other_two, small, small_other, norm_gains, shared_biases, cot_own),
+        limit=LIMITS[3], cost=22,
         scratch=[pltpu.VMEM((rows // TILES, units), bf16)],
         name="feed_forward",
     )
@@ -784,9 +870,9 @@
         attend_backward,
         [sds((3, width, part)), sds((3 * part + history, width), bf16), sds((half, history)),
          sds((half, history)), sds((16, width)), sds((16, width))],
-        (groups, counts, queries, keys, values, lse, context_grad, delta, tokens, resid_one, send_one,
+        (facts, queries, keys, values, lse, context_grad, delta, tokens, resid_one, send_one,
          other_one, table, series_own, sums, inner_sums),
-        in_specs=[SM] * 2 + [VM] * 14, limit=LIMITS[4],
+        limit=LIMITS[4], cost=22,
         scratch=[pltpu.VMEM((rows, width), bf16)] * 3,
         name="attend_backward",
     )
@@ -800,38 +886,33 @@
         (active, preact_grad, normed_low, feed_grad, context, attend_out, grads_other,
          outer_error[0], inner_error[0], mixer_error[0], outer_start[0].T, inner_start.T, mixer_start[0].T,
          output_near, output_other),
-        limit=LIMITS[5],
+        limit=LIMITS[5], cost=6,
         name="feed_matrices",
     )
-    attend_matrix, embed_matrix, left_partial, series_grad = call(
-        other_matrices,
-        [sds((3, width, part)), sds(embed_weight.shape), sds((8, 4096)), sds((half, windows, history))],
-        (groups, attend_near, send_three, other_three, turned(attend_error[0]), embed_error[0],
-         attend_start.transpose(0, 2, 1), embed_start.T, left_part, sums_near, sums_other,
-         series_near, series_other),
-        in_specs=[SM] + [VM] * 12, limit=LIMITS[6],
-        name="other_matrices",
-    )
-    matrices = (embed_matrix, outer_matrix, attend_matrix, inner_matrix, mixer_matrix)
     padded = max(128, -(-4096 // replicas // 128) * 128)
     total = padded * replicas
-    if total > 4096:
-        left_partial = jnp.pad(left_partial, ((0, 0), (0, total - 4096)))
-    left, right, mean = pl.pallas_call(
+    left, right, mean, attend_matrix, embed_matrix = pl.pallas_call(
         functools.partial(reduce_factors, replicas),
-        out_shape=[sds((8, 3328)), sds((8, 3328)), sds((8, 768))],
-        in_specs=[VM] * 6,
-        out_specs=[VM] * 3,
+        out_shape=[sds((8, 3328)), sds((8, 3328)), sds((8, 768)), sds((3, width, part)), sds(embed_weight.shape)],
+        in_specs=[VM] * 14,
+        out_specs=[VM] * 5,
         scratch_shapes=[
             pltpu.VMEM((8, total), f32), pltpu.VMEM((8, total), f32), pltpu.VMEM((8, total), f32),
+            pltpu.VMEM((8, total), f32),
             pltpu.VMEM((replicas, 8, padded), f32), pltpu.VMEM((replicas, 8, padded), f32),
             pltpu.SemaphoreType.DMA((4, replicas)), pltpu.SemaphoreType.DMA((4, replicas)),
         ],
         compiler_params=pltpu.CompilerParams(
-            collective_id=1, has_side_effects=True, vmem_limit_bytes=LIMITS[7] * MIB
+            collective_id=1, has_side_effects=True, vmem_limit_bytes=LIMITS[6] * MIB
         ),
+        cost_estimate=estimate(30),
         name="reduce_factors",
-    )(left_partial, *matrices)
+    )(
+        facts, attend_near, send_three, other_three, turned(attend_error[0]), embed_error[0],
+        attend_start.transpose(0, 2, 1), embed_start.T, left_part, sums_near, sums_other,
+        outer_matrix, inner_matrix, mixer_matrix,
+    )
+    matrices = (embed_matrix, outer_matrix, attend_matrix, inner_matrix, mixer_matrix)
 
     step_rate = base_rate * math.sqrt(replicas * 7 / (windows * rows))
     mixer_rate = step_rate * math.sqrt(width / max(width * 16 // rows, 1))
@@ -847,6 +928,8 @@
         embed_bias_moment, gains_moment, biases_moment, query_bias_moment, inner_bias_moment[None]
     )
     vector_specs = [whole(a) for a in vectors]
+    split = pl.BlockSpec((half // steps, history), lambda i: (i, 0))
+    split_out = pl.BlockSpec((half // steps, windows, history), lambda i: (i, 0, 0))
     factors = [
         sds((group_count, 8, history)), sds((8, 1024)), sds((8, 512)), sds((8, 512)), sds((8, 256)),
         sds((8, 512)), sds((8, 512)), sds((3, 8, part)), sds((8, 1024)), sds((8, 512)),
@@ -854,13 +937,15 @@
     found = pl.pallas_call(
         functools.partial(renew_all, step_rate, mixer_rate),
         grid=(steps,),
-        out_shape=[sds(a.shape) for a in matrices] * 3 + [sds(a.shape) for a in vectors] * 2 + factors,
-        in_specs=[whole(left), whole(right), whole(mean)] + specs * 3 + vector_specs * 2,
-        out_specs=specs * 3 + vector_specs * 2 + [whole(a) for a in factors],
-        compiler_params=pltpu.CompilerParams(vmem_limit_bytes=LIMITS[8] * MIB),
+        out_shape=[sds(a.shape) for a in matrices] * 3 + [sds(a.shape) for a in vectors] * 2
+        + factors + [sds(series.shape)],
+        in_specs=[whole(left), whole(right), whole(mean), split, split] + specs * 3 + vector_specs * 2,
+        out_specs=specs * 3 + vector_specs * 2 + [whole(a) for a in factors] + [split_out],
+        compiler_params=pltpu.CompilerParams(vmem_limit_bytes=LIMITS[7] * MIB),
+        cost_estimate=estimate(12),
         name="renew_all",
     )(
-        left, right, mean, *matrices,
+        left, right, mean, series_near, series_other, *matrices,
         embed_weight, outer_weight, turned(attend_weight), inner_weight, mixer_weight,
         embed_moment, outer_moment, turned(attend_moment), inner_moment, mixer_moment,
         *vectors, *vector_moments,
@@ -870,7 +955,7 @@
     lefts, rights = found[25:30], found[30:35]
     return (
         output,
-        series_grad,
+        found[35],
         weights[0],
         moments[0],
         errors[0][None],

time: 172 us -> 118 us (0.69)
  local copies, waits for them, and re-layouts: 26.5 us -> 3.91 us
  Pallas kernels: 133 us -> 111 us
  waiting for transfers between devices: 7.59 us -> 0.02 us
    unnamed x112 -> x76, local copies, waits for them, and re-layouts: 26.5 us -> 3.91 us
    pallas_call x7 -> x4, Pallas kernels: 85.7 us -> 63.2 us  [call(): pl.pallas_call(kernel, out_shape=outs, in_specs=in_specs if in_specs is n...]
    ppermute x8 -> x6, waiting for transfers between devices: 7.59 us -> 0.02 us  [swap(): return lax.ppermute(values, 'mp', [(0, 1), (1, 0)])]
    pallas_call x1, Pallas kernels: 16.6 us -> 10.6 us  [local(): pl.pallas_call(functools.partial(renew_all, step_rate, mixer_rate), grid=...]
    pallas_call x0 -> x1, Pallas kernels: none -> 5.83 us  [local(): pl.pallas_call(prepare, out_shape=[packed, packed, sds((half, history), b...]
  transfers between devices with their start and end apart: 8 -> 6, of which waited for: 2 -> 0; matrix products, arithmetic and copies ran while one was open for 0% -> 0% of each run, Pallas kernels for 30% -> 63%
where the time goes in v1:
time: 118 us
  Pallas kernels  111 us (94%)
  local copies, waits for them, and re-layouts  3.91 us (3%)
  starting transfers between devices  1.62 us (1%)
  between operations  1.44 us (1%)
    pallas_call x4, Pallas kernels, call(): pl.pallas_call(kernel, out_shape=outs, in_specs=in_specs if in_specs is n...  63.2 us
    pallas_call x1, Pallas kernels, local(): pl.pallas_call(functools.partial(reduce_factors, replicas), out_shape=[sd...  31.5 us
    pallas_call x1, Pallas kernels, local(): pl.pallas_call(functools.partial(renew_all, step_rate, mixer_rate), grid=...  10.6 us
    pallas_call x1, Pallas kernels, local(): pl.pallas_call(prepare, out_shape=[packed, packed, sds((half, history), b...  5.83 us
    unnamed x76, local copies, waits for them, and re-layouts  3.91 us
  transfers between devices with their start and end apart: 6, of which 0 were waited for; matrix products, arithmetic and copies ran while one was open for 0% of the time, Pallas kernels for 63%

profile of v1, /device:TPU:0, one launch (start us, length us, event | category | flops | bytes accessed | tf_op | source)
XLA Modules:
  0.0 118.1 jit_solution(2943015924701246923)
XLA Ops:
  0.7 5.8 %prepare.1 = (bf16[1232,512]{1,0:T(8,128)(2,1)S(1)}, bf16[1232,512]{1,0:T(8,128)(2,1)S(1)}, bf16[448,336]{1,0:T(8,128)(2,1)S(1)}, f32[8,1024]{1,0:T(8,128)S(1)},...) custom-call(s32[2]{0:T(128)} %groups_hbm.1, s32[2]{0:T(128)} %counts_hbm.1, ...), custom_call_target="tpu_custom_call" | custom-call | flops 7000000000 | bytes 14000000 | tf_op jit(solution)/shard_map/prepare/pallas_call | solution.py:816
  6.5 0.5 collective-permute-start
  7.1 14.8 %attend_forward.1 = (f32[896,512]{1,0:T(8,128)S(1)}, bf16[896,512]{1,0:T(8,128)(2,1)S(1)}, bf16[896,512]{1,0:T(8,128)(2,1)S(1)}, bf16[896,512]{1,0:T(8,128)(2,1)...) custom-call(s32[8,128]{1,0:T(8,128)S(1)} %get-tuple-element.118.fact, ...), custom_call_target="tpu_custom_call" | custom-call | flops 15000000512 | bytes 30000000 | tf_op jit(solution)/shard_map/attend_forward/pallas_call | solution.py:768
  21.9 20.3 %feed_forward.1 = (f32[448,512]{1,0:T(8,128)S(1)}, f32[448,512]{1,0:T(8,128)S(1)}, bf16[896,2048]{1,0:T(8,128)(2,1)S(1)}, bf16[896,2048]{1,0:T(8,128)(2,1)S(1)},...) custom-call(s32[8,128]{1,0:T(8,128)S(1)} %get-tuple-element.118.fact, ...), custom_call_target="tpu_custom_call" | custom-call | flops 22000001024 | bytes 44000000 | tf_op jit(solution)/shard_map/feed_forward/pallas_call | solution.py:768
  42.3 0.0 copy-start.30
  42.3 0.9 copy-done.30
  43.2 0.9 copy-done.32
  44.1 0.1 collective-permute-start.2
  44.2 0.4 collective-permute-start.1
  44.6 0.0 copy-start.17
  44.7 0.0 copy-start.33
  44.7 22.7 %attend_backward.1 = (f32[3,512,256]{2,1,0:T(8,128)S(1)}, bf16[1104,512]{1,0:T(8,128)(2,1)S(1)}, f32[448,336]{1,0:T(8,128)S(1)}, f32[448,336]{1,0:T(8,128)S(1)},...) custom-call(s32[8,128]{1,0:T(8,128)S(1)} %get-tuple-element.118.facts, bf16[896,512]{1,0:T(8,128)(2,1)S(1)} %get-tuple-element.137.query_ref, ...), custom_call_target="tpu_custom_call" | custom-call | flops 22000001024 | bytes 44000000 | tf_op jit(solution)/shard_map/attend_backward/pallas_call | solution.py:768
  67.4 0.8 copy-done.36
  68.2 0.1 collective-permute-start.3
  68.3 0.4 collective-permute-start.4
  68.8 0.1 collective-permute-start.5
  68.9 0.0 copy-start.6
  68.9 0.0 copy-start.9
  69.0 0.0 copy-start.19
  69.0 5.3 %feed_matrices.1 = (f32[1024,512]{1,0:T(8,128)S(1)}, f32[512,1024]{1,0:T(8,128)S(1)}, f32[256,512]{1,0:T(8,128)S(1)}, f32[8,1792]{1,0:T(8,128)S(1)}, f32[448,2,512]{2,1,0:T(2,128)}) custom-call(bf16[896,2048]{1,0:T(8,128)(2,1)S(1)} %get-tuple-element.128.active_ref, bf16[896,2048]{1,0:T(8,128)(2,1)S(1)} %get-tuple-element.129.preact_ref, ...), custom_call_target="tpu_custom_call" | custom-call | flops 6000000000 | bytes 12000000 | tf_op jit(solution)/shard_map/feed_matrices/pallas_call | solution.py:768
  74.3 0.0 copy-start.2
  74.5 31.5 %reduce_factors.1 = (f32[8,3328]{1,0:T(8,128)S(1)}, f32[8,3328]{1,0:T(8,128)S(1)}, f32[8,768]{1,0:T(8,128)S(1)}, f32[3,512,256]{2,1,0:T(8,128)S(1)}, f32[3,336,512]{2,1,0:T(8,128)S(1)}) custom-call(s32[8,128]{1,0:T(8,128)S(1)} %get-tuple-element.118.facts, f32[3,512,256]{2,1,0:T(8,128)S(1)} %get-tuple-element.148.near_attend, ...), custom_call_target="tpu_custom_call" | custom-call | flops 30000001024 | bytes 60000000 | tf_op jit(solution)/shard_map/reduce_factors/pallas_call | solution.py:894
  106.3 1.0 copy-done.35
  107.3 10.6 %renew_all.1 = (f32[3,336,512]{2,1,0:T(8,128)}, f32[1024,512]{1,0:T(8,128)}, f32[3,512,256]{2,1,0:T(8,128)}, f32[512,1024]{1,0:T(8,128)}, f32[256,512]{1,0:T(8,1...) custom-call(f32[8,3328]{1,0:T(8,128)S(1)} %get-tuple-element.156.lef, ...), custom_call_target="tpu_custom_call" | custom-call | flops 12000000000 | bytes 24000000 | tf_op jit(solution)/shard_map/renew_all/pallas_call | solution.py:937
  (71 shorter events, 0.2 us)
Async XLA Ops:
  6.5 15.4 %collective-permute-start = (bf16[2752,512]{1,0:T(8,128)(2,1)S(1)}, bf16[2752,512]{1,0:T(8,128)(2,1)S(1)}, u32[]{:S(2)}, u32[]{:S(2)}) collective-permute-start(bf16[2752,512]{1,0:T(8,128)(2,1)S(1)} %get-tuple-element.125.own), channel_id=1, source_target_pairs={{0,1},{1,0},{2,3},{3,2},{4,5},{5,4},{6,7},{7,6},{8,9},{9,8},{10,11... | collective-permute-start | bytes 8454152 | tf_op jit(solution)/shard_map/ppermute | solution.py:810
  44.1 24.7 %collective-permute-start.2 = (f32[448,512]{1,0:T(8,128)S(1)}, f32[448,512]{1,0:T(8,128)S(1)}, u32[]{:S(2)}, u32[]{:S(2)}) collective-permute-start(f32[448,512]{1,0:T(8,128)S(1)} %get-tuple-element.135), channel_id=1, source_target_pairs={{0,1},{1,0},{2,3},{3,2},{4,5},{5,4},{6,7},{7,6},{8,9},{9,8},{10,11... | collective-permute-start | bytes 2752520 | tf_op jit(solution)/shard_map/ppermute | solution.py:810
  44.2 24.6 %collective-permute-start.1 = (bf16[2304,512]{1,0:T(8,128)(2,1)S(1)}, bf16[2304,512]{1,0:T(8,128)(2,1)S(1)}, u32[]{:S(2)}, u32[]{:S(2)}) collective-permute-start(bf16[2304,512]{1,0:T(8,128)(2,1)S(1)} %get-tuple-element.133), channel_id=1, source_target_pairs={{0,1},{1,0},{2,3},{3,2},{4,5},{5,4},{6,7},{7,6},{8,9},{9,8},{10,11... | collective-permute-start | bytes 7077896 | tf_op jit(solution)/shard_map/ppermute | solution.py:810
  68.2 6.1 %collective-permute-start.3 = (bf16[1104,512]{1,0:T(8,128)(2,1)S(1)}, bf16[1104,512]{1,0:T(8,128)(2,1)S(1)}, u32[]{:S(2)}, u32[]{:S(2)}) collective-permute-start(bf16[1104,512]{1,0:T(8,128)(2,1)S(1)} %get-tuple-element.149.own), channel_id=1, source_target_pairs={{0,1},{1,0},{2,3},{3,2},{4,5},{5,4},{6,7},{7,6},{8,9},{9,8},{10,11... | collective-permute-start | bytes 3391496 | tf_op jit(solution)/shard_map/ppermute | solution.py:810
  68.3 6.0 %collective-permute-start.4 = (f32[16,512]{1,0:T(8,128)S(1)}, f32[16,512]{1,0:T(8,128)S(1)}, u32[]{:S(2)}, u32[]{:S(2)}) collective-permute-start(f32[16,512]{1,0:T(8,128)S(1)} %get-tuple-element.152), channel_id=1, source_target_pairs={{0,1},{1,0},{2,3},{3,2},{4,5},{5,4},{6,7},{7,6},{8,9},{9,8},{10,11... | collective-permute-start | bytes 98312 | tf_op jit(solution)/shard_map/ppermute | solution.py:810
  68.8 37.3 %collective-permute-start.5 = (f32[448,336]{1,0:T(8,128)S(1)}, f32[448,336]{1,0:T(8,128)S(1)}, u32[]{:S(2)}, u32[]{:S(2)}) collective-permute-start(f32[448,336]{1,0:T(8,128)S(1)} %get-tuple-element.160), channel_id=1, source_target_pairs={{0,1},{1,0},{2,3},{3,2},{4,5},{5,4},{6,7},{7,6},{8,9},{9,8},{10,11... | collective-permute-start | bytes 1806344 | tf_op jit(solution)/shard_map/ppermute | solution.py:810
  74.3 31.8 %copy-start.34 = (f32[256,512]{1,0:T(8,128)}, f32[256,512]{1,0:T(8,128)S(1)}, u32[]{:S(2)}) copy-start(f32[256,512]{1,0:T(8,128)S(1)} %get-tuple-element.155.mixer.refs_4_) | copy-start | bytes 1572868
  74.3 31.7 %copy-start.2 = (f32[512,1024]{1,0:T(8,128)S(1)}, f32[512,1024]{1,0:T(8,128)}, u32[]{:S(2)}) copy-start(f32[512,1024]{1,0:T(8,128)} %refs_8_.1) | copy-start | bytes 6291460
  74.3 31.7 %copy-start.3 = (f32[1024,512]{1,0:T(8,128)S(1)}, f32[1024,512]{1,0:T(8,128)}, u32[]{:S(2)}) copy-start(f32[1024,512]{1,0:T(8,128)} %refs_6_.1) | copy-start | bytes 6291460
  74.4 31.7 %copy-start.4 = (f32[1024,512]{1,0:T(8,128)S(1)}, f32[1024,512]{1,0:T(8,128)}, u32[]{:S(2)}) copy-start(f32[1024,512]{1,0:T(8,128)} %refs_11_.1) | copy-start | bytes 6291460
  74.4 31.7 %copy-start.5 = (f32[512,1024]{1,0:T(8,128)S(1)}, f32[512,1024]{1,0:T(8,128)}, u32[]{:S(2)}) copy-start(f32[512,1024]{1,0:T(8,128)} %refs_13_.1) | copy-start | bytes 6291460
  74.4 31.7 %copy-start.8 = (f32[3,336,512]{2,1,0:T(8,128)S(1)}, f32[3,336,512]{2,1,0:T(8,128)}, u32[]{:S(2)}) copy-start(f32[3,336,512]{2,1,0:T(8,128)} %refs_10_.1) | copy-start | bytes 6193156
  74.4 31.7 %copy-start.10 = (f32[512,3,256]{2,0,1:T(8,128)S(1)}, f32[512,3,256]{2,0,1:T(8,128)}, u32[]{:S(2)}) copy-start(f32[512,3,256]{2,0,1:T(8,128)} %param.42) | copy-start | bytes 4718596
  74.4 31.7 %copy-start.11 = (f32[512,3,256]{2,0,1:T(8,128)S(1)}, f32[512,3,256]{2,0,1:T(8,128)}, u32[]{:S(2)}) copy-start(f32[512,3,256]{2,0,1:T(8,128)} %param.43) | copy-start | bytes 4718596
  74.4 31.7 %copy-start.13 = (f32[256,512]{1,0:T(8,128)S(1)}, f32[256,512]{1,0:T(8,128)}, u32[]{:S(2)}) copy-start(f32[256,512]{1,0:T(8,128)} %refs_9_.1) | copy-start | bytes 1572868
  74.4 31.7 %copy-start.14 = (f32[256,512]{1,0:T(8,128)S(1)}, f32[256,512]{1,0:T(8,128)}, u32[]{:S(2)}) copy-start(f32[256,512]{1,0:T(8,128)} %refs_14_.1) | copy-start | bytes 1572868
  74.4 31.7 %copy-start.22 = (f32[3,512]{1,0:T(4,128)S(1)}, f32[3,512]{1,0:T(4,128)}, u32[]{:S(2)}) copy-start(f32[3,512]{1,0:T(4,128)} %refs_20_.1) | copy-start | bytes 18436
  74.5 31.7 %copy-start.23 = (f32[4,512]{1,0:T(4,128)S(1)}, f32[4,512]{1,0:T(4,128)}, u32[]{:S(2)}) copy-start(f32[4,512]{1,0:T(4,128)} %refs_22_.1) | copy-start | bytes 24580
  74.5 31.7 %copy-start.24 = (f32[1024]{0:T(1024)S(1)}, f32[1024]{0:T(1024)}, u32[]{:S(2)}) copy-start(f32[1024]{0:T(1024)} %param.62) | copy-start | bytes 12292
  74.5 31.7 %copy-start.26 = (f32[2,512]{1,0:T(2,128)S(1)}, f32[2,512]{1,0:T(2,128)}, u32[]{:S(2)}) copy-start(f32[2,512]{1,0:T(2,128)} %refs_21_.1) | copy-start | bytes 12292
  74.5 31.7 %copy-start.27 = (f32[1024]{0:T(1024)S(1)}, f32[1024]{0:T(1024)}, u32[]{:S(2)}) copy-start(f32[1024]{0:T(1024)} %param.63) | copy-start | bytes 12292
  74.5 31.7 %copy-start.28 = (f32[2,256]{1,0:T(2,128)S(1)}, f32[2,256]{1,0:T(2,128)}, u32[]{:S(2)}) copy-start(f32[2,256]{1,0:T(2,128)} %refs_18_.1) | copy-start | bytes 6148
  74.5 31.7 %copy-start.29 = (f32[2,256]{1,0:T(2,128)S(1)}, f32[2,256]{1,0:T(2,128)}, u32[]{:S(2)}) copy-start(f32[2,256]{1,0:T(2,128)} %refs_23_.1) | copy-start | bytes 6148
  74.5 31.7 %copy-start.37 = (f32[448,336]{1,0:T(8,128)S(1)}, f32[448,336]{1,0:T(8,128)}, u32[]{:S(2)}) copy-start(f32[448,336]{1,0:T(8,128)} %copy-done.36) | copy-start | bytes 1806340
  (20 other events, 261.6 us)
